TPU v7x, 256 devices: a whole 4x4x8 slice. The times are simulated.
256 devices in a mesh: seq: 64 (over x, z, core), dp: 4 (over y).
Axes of the slice: x: 4, y: 4, z: 8, core: 2. Of those that a mesh axis runs over, the one named last changes fastest.
Arguments:
- x_in: bfloat16 [4, 16384, 2048], P('dp', 'seq'), may hold values from -6 to 6
- gate_in: bfloat16 [4, 16384, 2048], P('dp', 'seq'), may hold values from -6 to 6
- keys_b: bfloat16 [4, 16384, 128], P('dp', 'seq'), may hold values from -6 to 6
- queries_c: bfloat16 [4, 16384, 128], P('dp', 'seq'), may hold values from -0.5 to 0.5
- decay_log: float32 [4, 32, 16384], P('dp', None, 'seq'), may hold values from -0.8 to 0
- level_mix: float32 [4, 15, 32, 16384], P('dp', None, None, 'seq'), may hold values from 0.2 to 2
- norm_gain: float32 [2048], replicated, may hold values from 0.25 to 1.75
- w_gate: bfloat16 [2048, 2816], P(None, ('seq', 'dp')), may hold values from -0.125 to 0.125
- w_up: bfloat16 [2048, 2816], P(None, ('seq', 'dp')), may hold values from -0.125 to 0.125
Outputs:
- hidden: bfloat16 [4, 16384, 2816], P('dp', 'seq')
All inputs are finite; a program needn't handle non-finite values.
Results may differ from a plain program's by a relative error of at most 0.0078.
Values may be sent and summed in bfloat16 or wider, within the bound.
No kernel may reach another device: no remote copies, remote signals or barrier semaphores. Data moves between devices by JAX's collectives and lax.ppermute only.
A program may use at most 128 MiB of HBM per device.

v0:
```python
import jax
import jax.numpy as jnp
from jax import lax
from jax.sharding import PartitionSpec as P

SPAN = 256
SPAN_BITS = 8


EPS = 1e-05
HIGH = lax.Precision.HIGHEST


def swapped(value, axis, distance):
    mask = 2**distance
    pairs = [(source, source ^ mask) for source in range(lax.axis_size(axis))]
    return lax.ppermute(value, axis, pairs)


def top_bit(values):
    powers = jnp.arange(1, 31, dtype=jnp.int32)
    return jnp.sum(values[..., None] >> powers > 0, axis=-1)


def block_inner(x_blk, b_blk, c_blk, a_blk, mix_low):
    length = a_blk.shape[1]
    inner_count = mix_low.shape[0]
    running = jnp.cumsum(a_blk, axis=1)
    position = jnp.arange(length, dtype=jnp.int32)
    differ = position[:, None] ^ position[None, :]
    level_table = jnp.where(differ > 0, top_bit(differ) + 1, 0)
    level_picks = (
        level_table[None] == jnp.arange(inner_count, dtype=jnp.int32)[:, None, None]
    ).astype(jnp.float32)
    chosen = jnp.einsum("lht,lts->hts", mix_low, level_picks, precision=HIGH)
    causal_mask = position[:, None] >= position[None, :]
    log_gap = jnp.where(causal_mask[None], running[:, :, None] - running[:, None, :], -jnp.inf)
    scores = jnp.dot(c_blk, b_blk.T, preferred_element_type=jnp.float32)
    weights = (chosen * jnp.exp(log_gap) * scores[None]).astype(jnp.bfloat16)
    local_part = jnp.einsum("hts,shp->thp", weights, x_blk, preferred_element_type=jnp.float32)
    tail_decay = jnp.exp(running[:, -1:] - running)
    scaled_keys = (tail_decay.T[:, :, None] * b_blk[:, None, :]).astype(jnp.bfloat16)
    block_state = jnp.einsum("shn,shp->hnp", scaled_keys, x_blk, preferred_element_type=jnp.float32)
    return (local_part, block_state, running)


def block_distant(c_blk, running, mix_high, levels):
    growth = jnp.exp(running)
    distant_sum = jnp.zeros((c_blk.shape[0], running.shape[0], levels[0].shape[2]), jnp.float32)
    for level_rank in range(len(levels)):
        level_scale = (mix_high[level_rank] * growth).T
        product = jnp.einsum(
            "tn,hnp->thp",
            c_blk,
            levels[level_rank].astype(jnp.bfloat16),
            preferred_element_type=jnp.float32,
        )
        distant_sum = distant_sum + level_scale[:, :, None] * product
    return distant_sum


def per_device(x_in, gate_in, keys_b, queries_c, decay_log, level_mix, norm_gain, w_gate, w_up):
    tok_dev = x_in.shape[1]
    embedding_width = x_in.shape[2]
    head_count = decay_log.shape[1]
    head_dim = embedding_width // head_count
    blocks = tok_dev // SPAN
    inner_count = SPAN_BITS + 1
    seq_bits = lax.axis_size("seq").bit_length() - 1
    x_blocks = x_in[0].reshape(blocks, SPAN, head_count, head_dim)
    b_blocks = keys_b[0].reshape(blocks, SPAN, -1)
    c_blocks = queries_c[0].reshape(blocks, SPAN, -1)
    a_blocks = decay_log[0].reshape(head_count, blocks, SPAN)
    mix_all = level_mix[0].reshape(level_mix.shape[1], head_count, blocks, SPAN)
    local_parts, block_states, block_decays, runnings = ([], [], [], [])
    block_index = 0
    local_part, block_state, running = block_inner(
        x_blocks[block_index],
        b_blocks[block_index],
        c_blocks[block_index],
        a_blocks[:, block_index],
        mix_all[:inner_count, :, block_index],
    )
    local_parts.append(local_part)
    block_states.append(block_state)
    block_decays.append(running[:, -1])
    runnings.append(running)
    summary = jnp.zeros_like(block_states[0])
    block_index = 0
    summary = (
        jnp.exp(block_decays[block_index])[:, None, None] * summary + block_states[block_index]
    )
    summary_decay = block_decays[block_index]
    rank_here = lax.axis_index("seq")
    own_prefix = jnp.zeros((head_count,), jnp.float32)
    device_levels = []
    for bit_index in range(seq_bits):
        other_state, other_decay = swapped((summary, summary_decay), "seq", bit_index)
        is_upper = rank_here >> bit_index & 1 == 1
        device_levels.append(
            jnp.where(is_upper, jnp.exp(own_prefix)[:, None, None] * other_state, 0.0)
        )
        lower_state = jnp.where(is_upper, other_state, summary)
        lower_decay = jnp.where(is_upper, other_decay, summary_decay)
        upper_state = jnp.where(is_upper, summary, other_state)
        upper_decay = jnp.where(is_upper, summary_decay, other_decay)
        summary = jnp.exp(upper_decay)[:, None, None] * lower_state + upper_state
        summary_decay = lower_decay + upper_decay
        own_prefix = jnp.where(is_upper, own_prefix + other_decay, own_prefix)
    zero_decay = jnp.zeros((head_count,), jnp.float32)
    block_index = 0
    levels = []
    lead_decay = sum(block_decays[:block_index], zero_decay)
    for device_level in device_levels:
        levels.append(jnp.exp(lead_decay)[:, None, None] * device_level)
    distant = block_distant(
        c_blocks[block_index], runnings[block_index], mix_all[inner_count:, :, block_index], levels
    )
    outputs = local_parts[block_index] + distant
    mixed = outputs.reshape(tok_dev, embedding_width)
    gated = mixed * jax.nn.silu(gate_in[0].astype(jnp.float32))
    normed = (
        gated * lax.rsqrt(jnp.mean(gated * gated, axis=-1, keepdims=True) + EPS) * norm_gain
    ).astype(jnp.bfloat16)
    paired = jnp.stack([w_gate, w_up])
    dp_count = lax.axis_size("dp")
    seq_count = lax.axis_size("seq")
    seq_weights = lax.all_gather(paired, "seq", axis=2, tiled=True)
    projected = jnp.einsum(
        "td,gdk->gtk",
        normed,
        lax.all_gather(seq_weights, "dp", axis=2, tiled=True),
        preferred_element_type=jnp.float32,
    )
    returned = (jax.nn.silu(projected[0]) * projected[1]).astype(jnp.bfloat16)
    hidden = (
        returned.reshape(tok_dev, dp_count, seq_count, -1)
        .transpose(0, 2, 1, 3)
        .reshape(tok_dev, -1)
    )
    return hidden[None]


def solution(mesh):
    in_specs = (
        P("dp", "seq", None),
        P("dp", "seq", None),
        P("dp", "seq", None),
        P("dp", "seq", None),
        P("dp", None, "seq"),
        P("dp", None, None, "seq"),
        P(),
        P(None, ("seq", "dp")),
        P(None, ("seq", "dp")),
    )
    out_specs = P("dp", "seq", None)
    return jax.shard_map(
        per_device, mesh=mesh, in_specs=in_specs, out_specs=out_specs, check_vma=False
    )
```

profile of v0, /device:TPU:1, one launch (start us, length us, event | category | flops | bytes accessed | tf_op | source)
XLA Modules:
  0.0 343.9 jit_solution(13174789039232599970)
XLA Ops:
  8.3 86.5 %all-gather.3.cloned.1.call-done = bf16[2,2048,704]{1,0,2:T(2,128)(2,1)} async-done(((bf16[2,2048,11]{1,0,2:T(2,128)(2,1)}), bf16[2,2048,704]{1,0,2:T(2,128)(2,1)}) %all-gather.3.cloned.1.call-update) | async-done | bytes 5767184 | tf_op jit(solution)/shard_map/all_gather | solution.py:128
  94.8 7.7 %copy.47 = bf16[2,2048,704]{1,2,0:T(8,128)(2,1)} copy(bf16[2,2048,704]{1,0,2:T(2,128)(2,1)} %all-gather.3.cloned.1.call-done) | data formatting | bytes 11534336 | tf_op jit(solution)/shard_map/all_gather | solution.py:128
  107.8 2.4 collective-permute-done
  113.1 23.1 %collective-permute-done.3 = f32[32]{0:T(128)S(1)} collective-permute-done((f32[32]{0:T(128)S(1)}, f32[32]{0:T(128)S(1)}, u32[]{:S(2)}, u32[]{:S(2)}) %collective-permute-start.3) | collective-permute-done | bytes 160 | tf_op jit(solution)/shard_map/ppermute | solution.py:17
  142.7 43.6 %collective-permute-done.5 = f32[32]{0:T(128)S(1)} collective-permute-done((f32[32]{0:T(128)S(1)}, f32[32]{0:T(128)S(1)}, u32[]{:S(2)}, u32[]{:S(2)}) %collective-permute-start.5) | collective-permute-done | bytes 160 | tf_op jit(solution)/shard_map/ppermute | solution.py:17
  186.2 2.8 select_add_fusion.2
  192.2 2.4 copy.58
  195.6 9.3 %fusion.1 = bf16[32,256,256]{2,0,1:T(8,128)(2,1)} fusion(f32[256,256]{1,0:T(8,128)} %fusion.58, f32[32,256]{1,0:T(8,128)S(1)} %copy_bitcast_fusion, f32[32,256]{0,1:T(8,128)} %copy.51, pred[256,256]{1,0:T(8,128)(4,1)} %iota_compare_fusion.4, f32[1,9,32,256]{2,1,3,0:T(8,128)} %copy.58, s32[256,256]{1,0:T(8,128)S(1)} %add_select_fusion), kind=kOutput, calls=%fused_computation.2 | convolution fusion | flops 237568000 | bytes 5144576 | tf_op jit(solution)/shard_map/lht,lts->hts/dot_general | solution.py:35
  204.9 3.6 %collective-permute-start.7 = (f32[32]{0:T(128)S(1)}, f32[32]{0:T(128)S(1)}, u32[]{:S(2)}, u32[]{:S(2)}) collective-permute-start(f32[32]{0:T(128)S(1)} %get-tuple-element.19), channel_id=1, source_target_pairs={{0,32},{4,36},{8,40},{12,44},{16,48},{20,52},{24,56},{28,60},{32,0... | collective-permute-start | bytes 392 | tf_op jit(solution)/shard_map/ppermute | solution.py:17
  208.5 30.9 %collective-permute-done.7 = f32[32]{0:T(128)S(1)} collective-permute-done((f32[32]{0:T(128)S(1)}, f32[32]{0:T(128)S(1)}, u32[]{:S(2)}, u32[]{:S(2)}) %collective-permute-start.7) | collective-permute-done | bytes 160 | tf_op jit(solution)/shard_map/ppermute | solution.py:17
  239.4 2.8 select_add_fusion.1
  242.4 4.7 %fusion.2 = f32[32,256,64]{1,2,0:T(8,128)S(1)} fusion(bf16[256,32,64]{0,2,1:T(8,128)(2,1)S(1)} %bitcast.171, bf16[32,256,256]{2,0,1:T(8,128)(2,1)} %fusion.1), kind=kOutput, calls=%fused_computation.6 | convolution fusion | flops 268435456 | bytes 7340032 | tf_op jit(solution)/shard_map/hts,shp->thp/dot_general | solution.py:40
  248.5 2.6 copy.55
  251.0 15.6 %collective-permute-done.9 = f32[32]{0:T(128)S(1)} collective-permute-done((f32[32]{0:T(128)S(1)}, f32[32]{0:T(128)S(1)}, u32[]{:S(2)}, u32[]{:S(2)}) %collective-permute-start.9) | collective-permute-done | bytes 160 | tf_op jit(solution)/shard_map/ppermute | solution.py:17
  274.6 19.5 %collective-permute-done.10 = f32[32,128,64]{1,2,0:T(8,128)S(1)} collective-permute-done((f32[32,128,64]{1,2,0:T(8,128)S(1)}, f32[32,128,64]{1,2,0:T(8,128)S(1)}, u32[]{:S(2)}, u32[]{:S(2)}) %collective-permute-start.10) | collective-permute-done | bytes 1048608 | tf_op jit(solution)/shard_map/ppermute | solution.py:17
  294.1 2.9 multiply_reduce_fusion
  297.1 2.0 copy.54
  299.1 8.5 %all-gather.5.cloned.1.call-done = bf16[2,2048,2816]{1,2,0:T(8,128)(2,1)} async-done(((bf16[2,2048,704]{1,2,0:T(8,128)(2,1)}), bf16[2,2048,2816]{1,2,0:T(8,128)(2,1)}) %all-gather.5.cloned.1.call-update) | async-done | bytes 23068688 | tf_op jit(solution)/shard_map/all_gather | solution.py:132
  307.6 11.6 %convolution_bitcast_fusion = f32[2,256,2816]{1,2,0:T(8,128)S(1)} fusion(bf16[2,2048,2816]{1,2,0:T(8,128)(2,1)} %all-gather.5.cloned.1.call-done, f32[256,2048]{1,0:T(8,128)S(1)} %copy.54, f32[2048]{0:T(1024)S(1)} %copy-done.24, f32[256]{0:T(256)S(1)} %add_rsqrt_fusion, bf16[1,256,2048]{2,1,0:T(8,128)(2,1)S(1)} %copy-done.12), kind=kOutput, calls=%fused_computation.5 | convolution fusion | flops 5910298624 | bytes 31990784 | tf_op jit(solution)/shard_map/td,gdk->gtk/dot_general | solution.py:129
  319.3 2.0 fusion.86
  321.2 4.5 %squeeze.40 = f32[256,4,64,11]{0,3,2,1:T(8,128)} reshape(f32[1,256,2816]{1,2,0:T(8,128)} %get-tuple-element.8) | data formatting | bytes 5767168 | tf_op jit(solution)/shard_map/squeeze | solution.py:135
  325.7 2.2 squeeze.41
  328.0 4.8 %fusion.23 = bf16[256,64,4,11]{0,3,1,2:T(8,128)(2,1)S(1)} fusion(f32[256,4,64,11]{0,3,2,1:T(8,128)} %squeeze.41, f32[256,4,64,11]{0,3,2,1:T(8,128)} %squeeze.40), kind=kLoop, calls=%fused_computation.39 | loop fusion | flops 4325376 | bytes 7208960 | tf_op jit(solution)/shard_map/transpose | solution.py:138
  334.6 2.5 copy.57
  (110 shorter events, 31.5 us)
Async XLA Ops:
  6.5 132.5 %copy-start = (bf16[1,256,128]{2,1,0:T(8,128)(2,1)S(1)}, bf16[1,256,128]{2,1,0:T(8,128)(2,1)}, u32[]{:S(2)}) copy-start(bf16[1,256,128]{2,1,0:T(8,128)(2,1)} %param.12) | copy-start | bytes 196612
  6.5 88.2 %all-gather.3.cloned.1.call-start = ((), (), s32[]{:S(2)}) async-start(), calls=%async_computation | async-start | bytes 5857280 | tf_op jit(solution)/shard_map/all_gather | solution.py:128
  8.2 299.4 %all-gather.5.cloned.1.call-start = ((), (), s32[]{:S(2)}) async-start(), calls=%async_computation.1 | async-start | bytes 28835840 | tf_op jit(solution)/shard_map/all_gather | solution.py:132
  104.3 1.7 collective-permute-start.1
  107.5 2.7 collective-permute-start
  111.5 24.7 %collective-permute-start.2 = (f32[32,128,64]{1,2,0:T(8,128)S(1)}, f32[32,128,64]{1,2,0:T(8,128)S(1)}, u32[]{:S(2)}, u32[]{:S(2)}) collective-permute-start(f32[32,128,64]{1,2,0:T(8,128)S(1)} %select_add_fusion.4), channel_id=1, source_target_pairs={{0,8},{4,12},{8,0},{12,4},{16,24},{20,28},{24,16},{28,20},{32,40},... | collective-permute-start | bytes 3145736 | tf_op jit(solution)/shard_map/ppermute | solution.py:17
  112.0 24.2 %collective-permute-start.3 = (f32[32]{0:T(128)S(1)}, f32[32]{0:T(128)S(1)}, u32[]{:S(2)}, u32[]{:S(2)}) collective-permute-start(f32[32]{0:T(128)S(1)} %get-tuple-element.23), channel_id=1, source_target_pairs={{0,8},{4,12},{8,0},{12,4},{16,24},{20,28},{24,16},{28,20},{32,40},... | collective-permute-start | bytes 392 | tf_op jit(solution)/shard_map/ppermute | solution.py:17
  137.6 48.7 %collective-permute-start.4 = (f32[32,128,64]{1,2,0:T(8,128)}, f32[32,128,64]{1,2,0:T(8,128)S(1)}, u32[]{:S(2)}, u32[]{:S(2)}) collective-permute-start(f32[32,128,64]{1,2,0:T(8,128)} %select_add_fusion.3), channel_id=1, source_target_pairs={{0,16},{4,20},{8,24},{12,28},{16,0},{20,4},{24,8},{28,12},{32,48},... | collective-permute-start | bytes 3145736 | tf_op jit(solution)/shard_map/ppermute | solution.py:17
  141.8 50.4 %slice-start = ((f32[1,15,32,256]{3,2,1,0:T(8,128)}), f32[1,9,32,256]{3,2,1,0:T(8,128)S(1)}, s32[]{:S(2)}) async-start(f32[1,15,32,256]{3,2,1,0:T(8,128)} %param.14), calls=%async_computation.2 | async-start | bytes 589824 | tf_op jit(solution)/shard_map/slice | solution.py:82
  141.8 44.4 %collective-permute-start.5 = (f32[32]{0:T(128)S(1)}, f32[32]{0:T(128)S(1)}, u32[]{:S(2)}, u32[]{:S(2)}) collective-permute-start(f32[32]{0:T(128)S(1)} %get-tuple-element.21), channel_id=1, source_target_pairs={{0,16},{4,20},{8,24},{12,28},{16,0},{20,4},{24,8},{28,12},{32,48},... | collective-permute-start | bytes 392 | tf_op jit(solution)/shard_map/ppermute | solution.py:17
  189.0 50.3 %collective-permute-start.6 = (f32[32,128,64]{1,2,0:T(8,128)}, f32[32,128,64]{1,2,0:T(8,128)S(1)}, u32[]{:S(2)}, u32[]{:S(2)}) collective-permute-start(f32[32,128,64]{1,2,0:T(8,128)} %select_add_fusion.2), channel_id=1, source_target_pairs={{0,32},{4,36},{8,40},{12,44},{16,48},{20,52},{24,56},{28,60},{32,0... | collective-permute-start | bytes 3145736 | tf_op jit(solution)/shard_map/ppermute | solution.py:17
  204.9 34.5 %collective-permute-start.7 = (f32[32]{0:T(128)S(1)}, f32[32]{0:T(128)S(1)}, u32[]{:S(2)}, u32[]{:S(2)}) collective-permute-start(f32[32]{0:T(128)S(1)} %get-tuple-element.19), channel_id=1, source_target_pairs={{0,32},{4,36},{8,40},{12,44},{16,48},{20,52},{24,56},{28,60},{32,0... | collective-permute-start | bytes 392 | tf_op jit(solution)/shard_map/ppermute | solution.py:17
  242.2 25.0 %collective-permute-start.8 = (f32[32,128,64]{1,2,0:T(8,128)}, f32[32,128,64]{1,2,0:T(8,128)}, u32[]{:S(2)}, u32[]{:S(2)}) collective-permute-start(f32[32,128,64]{1,2,0:T(8,128)} %select_add_fusion.1), channel_id=1, source_target_pairs={{0,64},{4,68},{8,72},{12,76},{16,80},{20,84},{24,88},{28,92},{32,9... | collective-permute-start | bytes 3145736 | tf_op jit(solution)/shard_map/ppermute | solution.py:17
  247.1 19.5 %copy-start.23 = (f32[32]{0:T(128)S(1)}, f32[32]{0:T(128)}, u32[]{:S(2)}) copy-start(f32[32]{0:T(128)} %copy-done.22) | copy-start | bytes 388
  247.1 19.6 %copy-start.6 = (f32[32,128,64]{1,2,0:T(8,128)S(1)}, f32[32,128,64]{1,2,0:T(8,128)}, u32[]{:S(2)}) copy-start(f32[32,128,64]{1,2,0:T(8,128)} %copy-done.5) | copy-start | bytes 3145732
  247.2 19.5 %collective-permute-start.9 = (f32[32]{0:T(128)S(1)}, f32[32]{0:T(128)S(1)}, u32[]{:S(2)}, u32[]{:S(2)}) collective-permute-start(f32[32]{0:T(128)S(1)} %get-tuple-element.17), channel_id=1, source_target_pairs={{0,64},{4,68},{8,72},{12,76},{16,80},{20,84},{24,88},{28,92},{32,9... | collective-permute-start | bytes 392 | tf_op jit(solution)/shard_map/ppermute | solution.py:17
  269.0 25.0 %collective-permute-start.10 = (f32[32,128,64]{1,2,0:T(8,128)S(1)}, f32[32,128,64]{1,2,0:T(8,128)S(1)}, u32[]{:S(2)}, u32[]{:S(2)}) collective-permute-start(f32[32,128,64]{1,2,0:T(8,128)S(1)} %select_add_fusion), channel_id=1, source_target_pairs={{0,128},{4,132},{8,136},{12,140},{16,144},{20,148},{24,152},{28,15... | collective-permute-start | bytes 3145736 | tf_op jit(solution)/shard_map/ppermute | solution.py:17
  272.7 21.4 %copy-start.2 = (f32[1,256,2048]{1,2,0:T(8,128)S(1)}, f32[1,256,2048]{1,2,0:T(8,128)}, u32[]{:S(2)}) copy-start(f32[1,256,2048]{1,2,0:T(8,128)} %copy.55) | copy-start | bytes 6291460
  272.7 21.4 %copy-start.15 = (f32[256,32]{0,1:T(8,128)S(1)}, f32[256,32]{0,1:T(8,128)}, u32[]{:S(2)}) copy-start(f32[256,32]{0,1:T(8,128)} %get-tuple-element.10) | copy-start | bytes 98308
  272.7 21.4 %copy-start.16 = (f32[256,32]{0,1:T(8,128)S(1)}, f32[256,32]{0,1:T(8,128)}, u32[]{:S(2)}) copy-start(f32[256,32]{0,1:T(8,128)} %get-tuple-element.11) | copy-start | bytes 98308
  272.7 21.4 %copy-start.17 = (f32[256,32]{0,1:T(8,128)S(1)}, f32[256,32]{0,1:T(8,128)}, u32[]{:S(2)}) copy-start(f32[256,32]{0,1:T(8,128)} %get-tuple-element.12) | copy-start | bytes 98308
  272.7 21.4 %copy-start.18 = (f32[256,32]{0,1:T(8,128)S(1)}, f32[256,32]{0,1:T(8,128)}, u32[]{:S(2)}) copy-start(f32[256,32]{0,1:T(8,128)} %get-tuple-element.13) | copy-start | bytes 98308
  272.7 21.4 %copy-start.19 = (f32[256,32]{0,1:T(8,128)S(1)}, f32[256,32]{0,1:T(8,128)}, u32[]{:S(2)}) copy-start(f32[256,32]{0,1:T(8,128)} %get-tuple-element.14) | copy-start | bytes 98308
  272.7 21.4 %copy-start.20 = (f32[256,32]{0,1:T(8,128)S(1)}, f32[256,32]{0,1:T(8,128)}, u32[]{:S(2)}) copy-start(f32[256,32]{0,1:T(8,128)} %get-tuple-element.15) | copy-start | bytes 98308
  (15 other events, 63.1 us)
Sparse Core Ops, SparseCore 0:
  10.1 84.6 all-gather.2
  102.6 204.9 all-gather.4
where the time goes:
time: 344 us
  waiting for transfers between devices  230 us (67%)
  matrix products  34.5 us (10%)
  local copies, waits for them, and re-layouts  32.7 us (10%)
  other arithmetic  19.7 us (6%)
  between operations  13.8 us (4%)
  starting transfers between devices  13 us (4%)
    ppermute x11, waiting for transfers between devices, swapped(): return lax.ppermute(value, axis, pairs)  135 us
    all_gather x1, waiting for transfers between devices, per_device(): seq_weights = lax.all_gather(paired, 'seq', axis=2, tiled=True)  86.5 us
    ppermute x11, starting transfers between devices, swapped(): return lax.ppermute(value, axis, pairs)  13 us
    dot_general x1, matrix products, per_device(): jnp.einsum('td,gdk->gtk', normed, lax.all_gather(seq_weights, 'dp', axis=...  11.6 us
    dot_general x1, matrix products, block_inner(): chosen = jnp.einsum('lht,lts->hts', mix_low, level_picks, precision=HIGH)  9.28 us
    add x5, other arithmetic, per_device(): summary = jnp.exp(upper_decay)[:, None, None] * lower_state + upper_state  9.02 us
    all_gather x1, waiting for transfers between devices, per_device(): lax.all_gather(seq_weights, 'dp', axis=2, tiled=True)  8.55 us
    all_gather x1, local copies, waits for them, and re-layouts, per_device(): seq_weights = lax.all_gather(paired, 'seq', axis=2, tiled=True)  7.71 us
  transfers between devices with their start and end apart: 13, of which 8 were waited for; matrix products, arithmetic and copies ran while one was open for 13% of the time, Pallas kernels for 0%

commit v1 on v0

v1 whole, which is shorter than its diff:
```python
import jax
import jax.numpy as jnp
from jax import lax
from jax.sharding import Mesh
from jax.sharding import PartitionSpec as P

SPAN = 256
SPAN_BITS = 8
EPS = 1e-05
HIGH = lax.Precision.HIGHEST
SEQ = ("x", "z", "core")
STEPS = (("z", 1), ("z", 2), ("z", 4), ("x", 1), ("x", 2))
HEAD_DIM = 64


def swapped(value, axis, mask):
    return lax.ppermute(value, axis, [(i, i ^ mask) for i in range(lax.axis_size(axis))])


def shifted(value, axis, step):
    count = lax.axis_size(axis)
    return lax.ppermute(value, axis, [(i, (i + step) % count) for i in range(count)])


def top_bit(values):
    powers = jnp.arange(1, 31, dtype=jnp.int32)
    return jnp.sum(values[..., None] >> powers > 0, axis=-1)


def local_mix(x_blk, b_blk, c_blk, running, mix_low):
    length = running.shape[1]
    inner_count = mix_low.shape[0]
    position = jnp.arange(length, dtype=jnp.int32)
    differ = position[:, None] ^ position[None, :]
    level_table = jnp.where(differ > 0, top_bit(differ) + 1, 0)
    level_picks = (
        level_table[None] == jnp.arange(inner_count, dtype=jnp.int32)[:, None, None]
    ).astype(jnp.float32)
    chosen = jnp.einsum("lht,lts->hts", mix_low, level_picks, precision=HIGH)
    causal_mask = position[:, None] >= position[None, :]
    log_gap = jnp.where(causal_mask[None], running[:, :, None] - running[:, None, :], -jnp.inf)
    scores = jnp.dot(c_blk, b_blk.T, preferred_element_type=jnp.float32)
    weights = (chosen * jnp.exp(log_gap) * scores[None]).astype(jnp.bfloat16)
    return jnp.einsum("hts,shp->thp", weights, x_blk, preferred_element_type=jnp.float32)


def packed(state, decay, kind):
    heads, width, size = state.shape
    top = lax.reduce_precision(decay, 8, 7)
    middle = lax.reduce_precision(decay - top, 8, 7)
    low = lax.reduce_precision(decay - top - middle, 8, 7)
    tail = jnp.stack([top, middle, low] + [jnp.zeros_like(top)] * 5)
    tail = jnp.pad(tail, ((0, 0), (0, size - decay.shape[0])))
    rows = jnp.concatenate([state.reshape(heads * width, size), tail])
    return rows.astype(kind)


def unpacked(rows, heads):
    size = rows.shape[1]
    tail = rows[-8:, :heads].astype(jnp.float32)
    state = rows[:-8].reshape(-1, HEAD_DIM, size)
    return state.astype(jnp.float32), tail[0] + tail[1] + tail[2]


def gathered_weights(w_gate, w_up, core, row):
    gate, up = w_gate.T, w_up.T
    keep = jnp.where(core == 0, gate, up)
    other = swapped(jnp.where(core == 0, up, gate), "core", 1)
    pair = jnp.stack([jnp.where(core == 0, keep, other), jnp.where(core == 0, other, keep)])
    ring = [pair, shifted(pair, "dp", -1), shifted(pair, "dp", 2), shifted(pair, "dp", 1)]
    placed = []
    for index in range(4):
        turn = (index - row) % 4
        value = ring[0]
        for step in range(1, 4):
            value = jnp.where(turn == step, ring[step], value)
        placed.append(value)
    block = jnp.stack(placed, axis=1).reshape(-1, gate.shape[1])
    return lax.all_gather(block, ("x", "z"), axis=0, tiled=True)


def per_device(x_in, gate_in, keys_b, queries_c, decay_log, level_mix, norm_gain, w_gate, w_up):
    tokens, width = x_in.shape[1:]
    heads = decay_log.shape[1]
    head_dim = HEAD_DIM
    inner = SPAN_BITS + 1
    core = lax.axis_index("core")
    here = (lax.axis_index("x") * lax.axis_size("z") + lax.axis_index("z")) * 2 + core
    mine = gathered_weights(w_gate, w_up, core, lax.axis_index("dp"))
    other = swapped(mine, "core", 1)

    x_blk = x_in[0].reshape(tokens, heads, head_dim)
    b_blk, c_blk = keys_b[0], queries_c[0]
    mix = level_mix[0]
    running = jnp.cumsum(decay_log[0], axis=1)
    decay = running[:, -1]
    tail_decay = jnp.exp(running[:, -1:] - running)
    scaled_keys = (tail_decay.T[:, :, None] * b_blk[:, None, :]).astype(jnp.bfloat16)
    state = jnp.einsum("shn,shp->hpn", scaled_keys, x_blk, preferred_element_type=jnp.float32)

    half = heads // 2
    their_state, their_decay = unpacked(swapped(packed(state, decay, jnp.float32), "core", 1), heads)
    first_level = their_state.astype(jnp.bfloat16)
    lower_state = jnp.where(core == 0, state, their_state)
    upper_state = jnp.where(core == 0, their_state, state)
    upper_decay = jnp.where(core == 0, their_decay, decay)
    summary = jnp.exp(upper_decay)[:, None, None] * lower_state + upper_state
    summary = lax.dynamic_slice_in_dim(summary, core * half, half)
    total = decay + their_decay
    prefix = jnp.zeros_like(total)
    upper, lead = [core == 1], [prefix]
    prefix = jnp.where(core == 1, their_decay, 0.0)
    levels = []
    for bit, (axis, mask) in enumerate(STEPS, 1):
        received = swapped(packed(summary, total, jnp.bfloat16), axis, mask)
        levels.append(received[:-8])
        their_state, their_decay = unpacked(received, heads)
        is_upper = here >> bit & 1 == 1
        upper.append(is_upper)
        lead.append(prefix)
        if bit < len(STEPS):
            lower_state = jnp.where(is_upper, their_state, summary)
            upper_state = jnp.where(is_upper, summary, their_state)
            upper_decay = jnp.where(is_upper, total, their_decay)
            gain = lax.dynamic_slice_in_dim(jnp.exp(upper_decay), core * half, half)
            summary = gain[:, None, None] * lower_state + upper_state
            prefix = jnp.where(is_upper, prefix + their_decay, prefix)
            total = total + their_decay

    def whole(own):
        own = jnp.stack(own).reshape(len(own), half, head_dim, -1)
        theirs = swapped(own, "core", 1)
        pair = (jnp.where(core == 0, own, theirs), jnp.where(core == 0, theirs, own))
        return list(jnp.concatenate(pair, axis=1))

    all_levels = [first_level] + whole(levels[:3]) + whole(levels[3:])
    mixed = local_mix(x_blk, b_blk, c_blk, running, mix[:inner])
    for rank, level in enumerate(all_levels):
        growth = jnp.where(upper[rank], jnp.exp(running + lead[rank][:, None]), 0.0)
        scale = (mix[inner + rank] * growth).T
        product = jnp.einsum("tn,hpn->thp", c_blk, level, preferred_element_type=jnp.float32)
        mixed = mixed + scale[:, :, None] * product
    mixed = mixed.reshape(tokens, width)
    gated = mixed * jax.nn.silu(gate_in[0].astype(jnp.float32))
    normed = (
        gated * lax.rsqrt(jnp.mean(gated * gated, axis=-1, keepdims=True) + EPS) * norm_gain
    ).astype(jnp.bfloat16)
    dims = (((1,), (1,)), ((), ()))
    own_part = lax.dot_general(normed, mine, dims, preferred_element_type=jnp.float32)
    other_part = lax.dot_general(normed, other, dims, preferred_element_type=jnp.float32)
    gate_pre = jnp.where(core == 0, own_part, other_part)
    up_pre = jnp.where(core == 0, other_part, own_part)
    return (jax.nn.silu(gate_pre) * up_pre).astype(jnp.bfloat16)[None]


def solution(mesh):
    whole = Mesh(mesh.devices.reshape(4, 8, 2, 4), ("x", "z", "core", "dp"))
    in_specs = (
        P("dp", SEQ, None),
        P("dp", SEQ, None),
        P("dp", SEQ, None),
        P("dp", SEQ, None),
        P("dp", None, SEQ),
        P("dp", None, None, SEQ),
        P(),
        P(None, SEQ + ("dp",)),
        P(None, SEQ + ("dp",)),
    )
    return jax.shard_map(
        per_device, mesh=whole, in_specs=in_specs, out_specs=P("dp", SEQ, None), check_vma=False
    )
```

time: 344 us -> 233 us (0.68)
  waiting for transfers between devices: 230 us -> 140 us
  local copies, waits for them, and re-layouts: 32.7 us -> 14.2 us
  other arithmetic: 19.7 us -> 11.3 us
    ppermute x11 -> x13, waiting for transfers between devices: 135 us -> 36.9 us  [the longest x10 28.2 us: swapped(): lax.ppermute(value, axis, [(i, i ^ mask) for i in range(lax.axis_size(axi...]
    add x9 -> x0, other arithmetic: 9.04 us -> none  [the longest x5 9.02 us: per_device(): summary = jnp.exp(upper_decay)[:, None, None] * lower_state + upper_state]
    all_gather x2 -> x1, waiting for transfers between devices: 95.1 us -> 103 us  [gathered_weights(): return lax.all_gather(block, ('x', 'z'), axis=0, tiled=True)]
    all_gather x1 -> x0, local copies, waits for them, and re-layouts: 7.71 us -> none  [per_device(): seq_weights = lax.all_gather(paired, 'seq', axis=2, tiled=True)]
    squeeze x2 -> x0, local copies, waits for them, and re-layouts: 6.71 us -> none  [per_device(): returned = (jax.nn.silu(projected[0]) * projected[1]).astype(jnp.bfloat16)]
    transpose x2, other arithmetic: 5.57 us -> 0.2 us  [the longest x1 0.11 us: per_device(): scale = (mix[inner + rank] * growth).T]
    another operation x5 -> x13, local copies, waits for them, and re-layouts: 5.48 us -> 0.34 us  [the longest x6 0.19 us: packed(): tail = jnp.stack([top, middle, low] + [jnp.zeros_like(top)] * 5)]
    ppermute x11 -> x13, starting transfers between devices: 13 us -> 16 us  [the longest x10 13.8 us: swapped(): lax.ppermute(value, axis, [(i, i ^ mask) for i in range(lax.axis_size(axi...]
  transfers between devices with their start and end apart: 13 -> 14, of which waited for: 8 -> 9; matrix products, arithmetic and copies ran while one was open for 13% -> 21% of each run, Pallas kernels for 0% -> 0%
where the time goes in v1:
time: 233 us; the launch traced here: 232 us
  waiting for transfers between devices  140 us (60%)
  matrix products  36.4 us (16%)
  starting transfers between devices  16 us (7%)
  local copies, waits for them, and re-layouts  14.2 us (6%)
  between operations  14 us (6%)
  other arithmetic  11.3 us (5%)
    all_gather x1, waiting for transfers between devices, gathered_weights(): return lax.all_gather(block, ('x', 'z'), axis=0, tiled=True)  103 us
    ppermute x10, waiting for transfers between devices, swapped(): lax.ppermute(value, axis, [(i, i ^ mask) for i in range(lax.axis_size(axi...  28.2 us
    ppermute x10, starting transfers between devices, swapped(): lax.ppermute(value, axis, [(i, i ^ mask) for i in range(lax.axis_size(axi...  13.8 us
    dot_general x1, matrix products, per_device(): lax.dot_general(normed, other, dims, preferred_element_type=jnp.float32)  9.6 us
    ppermute x3, waiting for transfers between devices, shifted(): lax.ppermute(value, axis, [(i, (i + step) % count) for i in range(count)])  8.69 us
    dot_general x1, matrix products, local_mix(): chosen = jnp.einsum('lht,lts->hts', mix_low, level_picks, precision=HIGH)  7.43 us
    dot_general x1, matrix products, per_device(): lax.dot_general(normed, mine, dims, preferred_element_type=jnp.float32)  6.88 us
    dot_general x6, matrix products, per_device(): jnp.einsum('tn,hpn->thp', c_blk, level, preferred_element_type=jnp.float32)  5.19 us
  transfers between devices with their start and end apart: 14, of which 9 were waited for; matrix products, arithmetic and copies ran while one was open for 21% of the time, Pallas kernels for 0%

profile of v1, /device:TPU:1, one launch (start us, length us, event | category | flops | bytes accessed | tf_op | source)
XLA Modules:
  0.0 232.2 jit_solution(12388118878062835489)
XLA Ops:
  7.4 3.3 %collective-permute-start.8 = (bf16[11,2048]{1,0:T(8,128)(2,1)S(1)}, bf16[11,2048]{1,0:T(8,128)(2,1)S(1)}, u32[]{:S(2)}, u32[]{:S(2)}) collective-permute-start(bf16[11,2048]{1,0:T(8,128)(2,1)S(1)} %select_bitcast_fusion.4), channel_id=1, source_target_pairs={{0,4},{4,0},{1,5},{5,1},{2,6},{6,2},{3,7},{7,3},{8,12},{12,8},{9,1... | collective-permute-start | bytes 135176 | tf_op jit(solution)/shard_map/ppermute | solution.py:17
  14.7 2.7 %collective-permute-done.11 = bf16[2,11,2048]{2,1,0:T(8,128)(2,1)S(1)} collective-permute-done((bf16[2,11,2048]{2,1,0:T(8,128)(2,1)S(1)}, bf16[2,11,2048]{2,1,0:T(8,128)(2,1)S(1)}, u32[]{:S(2)}, u32[]{:S(2)}) %collective-permute-start.11) | collective-permute-done | bytes 90144 | tf_op jit(solution)/shard_map/ppermute | solution.py:22
  17.4 2.2 collective-permute-done.10
  19.6 3.8 %collective-permute-done.9 = bf16[2,11,2048]{2,1,0:T(8,128)(2,1)S(1)} collective-permute-done((bf16[2,11,2048]{2,1,0:T(8,128)(2,1)S(1)}, bf16[2,11,2048]{2,1,0:T(8,128)(2,1)S(1)}, u32[]{:S(2)}, u32[]{:S(2)}) %collective-permute-start.9) | collective-permute-done | bytes 90144 | tf_op jit(solution)/shard_map/ppermute | solution.py:22
  26.4 1.4 fusion.5
  30.3 1.6 collective-permute-done
  33.0 1.6 collective-permute-start.1
  35.8 103.3 %all-gather.2.cloned.1.call-done = bf16[2816,2048]{1,0:T(8,128)(2,1)} async-done(((bf16[88,2048]{1,0:T(8,128)(2,1)}), bf16[2816,2048]{1,0:T(8,128)(2,1)}) %all-gather.2.cloned.1.call-update) | async-done | bytes 11534352 | tf_op jit(solution)/shard_map/all_gather | solution.py:79
  141.2 2.5 %copy.30 = f32[1,9,32,256]{2,1,3,0:T(8,128)} copy(f32[1,9,32,256]{3,2,1,0:T(8,128)S(1)} %slice-done) | data formatting | bytes 589824
  143.8 11.3 %collective-permute-done.2 = bf16[1032,128]{1,0:T(8,128)(2,1)S(1)} collective-permute-done((bf16[1032,128]{1,0:T(8,128)(2,1)S(1)}, bf16[1032,128]{1,0:T(8,128)(2,1)S(1)}, u32[]{:S(2)}, u32[]{:S(2)}) %collective-permute-start.2) | collective-permute-done | bytes 264224 | tf_op jit(solution)/shard_map/ppermute | solution.py:17
  155.7 3.0 %collective-permute-start.3 = (bf16[1032,128]{1,0:T(8,128)(2,1)S(1)}, bf16[1032,128]{1,0:T(8,128)(2,1)S(1)}, u32[]{:S(2)}, u32[]{:S(2)}) collective-permute-start(bf16[1032,128]{1,0:T(8,128)(2,1)S(1)} %fusion.61), channel_id=1, source_target_pairs={{0,32},{8,40},{16,48},{24,56},{32,0},{40,8},{48,16},{56,24},{1,33}... | collective-permute-start | bytes 792584 | tf_op jit(solution)/shard_map/ppermute | solution.py:17
  158.7 7.4 %fusion.1 = bf16[32,256,256]{2,0,1:T(8,128)(2,1)} fusion(f32[256,256]{1,0:T(8,128)S(1)} %copy-done.10, f32[32,256]{1,0:T(8,128)S(1)} %copy_bitcast_fusion, f32[32,256]{0,1:T(8,128)S(1)} %copy.24, pred[256,256]{1,0:T(8,128)(4,1)S(1)} %iota_compare_fusion.6, f32[1,9,32,256]{2,1,3,0:T(8,128)S(1)} %copy-done.5, s32[256,256]{1,0:T(8,128)S(1)} %add_select_fusion), kind=kOutput, calls=%fused_computation.2 | convolution fusion | flops 237568000 | bytes 5144576 | tf_op jit(solution)/shard_map/lht,lts->hts/dot_general | solution.py:39
  166.2 7.3 %collective-permute-done.3 = bf16[1032,128]{1,0:T(8,128)(2,1)S(1)} collective-permute-done((bf16[1032,128]{1,0:T(8,128)(2,1)S(1)}, bf16[1032,128]{1,0:T(8,128)(2,1)S(1)}, u32[]{:S(2)}, u32[]{:S(2)}) %collective-permute-start.3) | collective-permute-done | bytes 264224 | tf_op jit(solution)/shard_map/ppermute | solution.py:17
  174.5 5.0 %fusion.2 = f32[32,256,64]{1,2,0:T(8,128)S(1)} fusion(bf16[256,32,64]{0,2,1:T(8,128)(2,1)} %bitcast.281, bf16[32,256,256]{2,0,1:T(8,128)(2,1)} %fusion.1), kind=kOutput, calls=%fused_computation.5 | convolution fusion | flops 268435456 | bytes 7340032 | tf_op jit(solution)/shard_map/hts,shp->thp/dot_general | solution.py:44
  179.5 2.7 %copy.28 = f32[1,256,2048]{1,2,0:T(8,128)} copy(bf16[1,256,2048]{2,1,0:T(8,128)(2,1)} %param.10) | data formatting | bytes 3145728 | tf_op jit(solution)/shard_map/convert_element_type | solution.py:144
  182.2 2.1 slice.204
  188.7 1.9 collective-permute-start.6
  191.2 7.1 %collective-permute-done.6 = bf16[1032,128]{1,0:T(8,128)(2,1)S(1)} collective-permute-done((bf16[1032,128]{1,0:T(8,128)(2,1)S(1)}, bf16[1032,128]{1,0:T(8,128)(2,1)S(1)}, u32[]{:S(2)}, u32[]{:S(2)}) %collective-permute-start.6) | collective-permute-done | bytes 264224 | tf_op jit(solution)/shard_map/ppermute | solution.py:17
  199.5 1.3 broadcast_select_fusion.1
  202.6 1.1 copy-done.2
  203.8 3.0 %multiply_reduce_fusion = (f32[256]{0:T(256)S(1)}, f32[256,32,64]{0,2,1:T(8,128)}) fusion(f32[256,32,64]{0,2,1:T(8,128)S(1)} %bitcast.270, bf16[1,256,128]{2,1,0:T(8,128)(2,1)S(1)} %copy-done, bf16[2,16,64,128]{3,2,1,0:T(8,128)(2,1)S(1)} %get-tuple-element.34, bf16[2,16,64,128]{3,2,1,0:T(8,128)(2,1)S(1)} %get-tuple-element.35, ...), kind=kOutput, calls=%fused_computation.33 | convolution fusion | flops 144441088 | bytes 18088960 | tf_op jit(solution)/shard_map/tn,hpn->thp/dot_general | solution.py:141
  206.8 2.0 copy.27
  208.8 6.9 %fusion.105 = f32[256,2816]{1,0:T(8,128)S(1)} fusion(bf16[2816,2048]{1,0:T(8,128)(2,1)} %all-gather.2.cloned.1.call-done, f32[256,2048]{1,0:T(8,128)S(1)} %copy.27, f32[2048]{0:T(1024)S(1)} %copy-done.28, f32[256]{0:T(256)S(1)} %add_rsqrt_fusion, bf16[1,256,2048]{2,1,0:T(8,128)(2,1)S(1)} %copy-done.8), kind=kOutput, calls=%fused_computation.216 | convolution fusion | flops 2957508608 | bytes 17572864 | tf_op jit(solution)/shard_map/dot_general | solution.py:149
  215.7 9.6 %fusion.23 = bf16[1,256,2816]{2,1,0:T(8,128)(2,1)} fusion(f32[256,2816]{1,0:T(8,128)S(1)} %fusion.105, pred[]{:T(512)S(6)} %eq.88, bf16[2816,2048]{1,0:T(8,128)(2,1)} %collective-permute-done.12, f32[256,2048]{1,0:T(8,128)S(1)} %copy.27, f32[2048]{0:T(1024)S(1)} %copy-done.28, f32[256]{0:T(256)S(1)} %add_rsqrt_fusion, bf16[1,256,2048]{2,1,0:T(8,128)(2,1)S(1)} %copy-done.8), kind=kOutput, calls=%fused_computation.42 | convolution fusion | flops 2963275776 | bytes 19014656 | tf_op jit(solution)/shard_map/dot_general | solution.py:150
  (164 shorter events, 24.0 us)
Async XLA Ops:
  6.5 22.9 %copy-start = (bf16[1,256,128]{2,1,0:T(8,128)(2,1)S(1)}, bf16[1,256,128]{2,1,0:T(8,128)(2,1)}, u32[]{:S(2)}) copy-start(bf16[1,256,128]{2,1,0:T(8,128)(2,1)} %param.12) | copy-start | bytes 196612
  6.5 132.6 %all-gather.2.cloned.1.call-start = ((), (), s32[]{:S(2)}) async-start(), calls=%async_computation | async-start | bytes 11894784 | tf_op jit(solution)/shard_map/all_gather | solution.py:79
  7.4 4.2 %collective-permute-start.8 = (bf16[11,2048]{1,0:T(8,128)(2,1)S(1)}, bf16[11,2048]{1,0:T(8,128)(2,1)S(1)}, u32[]{:S(2)}, u32[]{:S(2)}) collective-permute-start(bf16[11,2048]{1,0:T(8,128)(2,1)S(1)} %select_bitcast_fusion.4), channel_id=1, source_target_pairs={{0,4},{4,0},{1,5},{5,1},{2,6},{6,2},{3,7},{7,3},{8,12},{12,8},{9,1... | collective-permute-start | bytes 135176 | tf_op jit(solution)/shard_map/ppermute | solution.py:17
  12.5 4.8 %collective-permute-start.11 = (bf16[2,11,2048]{2,1,0:T(8,128)(2,1)S(1)}, bf16[2,11,2048]{2,1,0:T(8,128)(2,1)S(1)}, u32[]{:S(2)}, u32[]{:S(2)}) collective-permute-start(bf16[2,11,2048]{2,1,0:T(8,128)(2,1)S(1)} %pad_maximum_fusion.5), channel_id=1, source_target_pairs={{0,3},{1,0},{2,1},{3,2},{4,7},{5,4},{6,5},{7,6},{8,11},{9,8},{10,9... | collective-permute-start | bytes 270344 | tf_op jit(solution)/shard_map/ppermute | solution.py:22
  13.6 5.9 %collective-permute-start.10 = (bf16[2,11,2048]{2,1,0:T(8,128)(2,1)S(1)}, bf16[2,11,2048]{2,1,0:T(8,128)(2,1)S(1)}, u32[]{:S(2)}, u32[]{:S(2)}) collective-permute-start(bf16[2,11,2048]{2,1,0:T(8,128)(2,1)S(1)} %pad_maximum_fusion.5), channel_id=1, source_target_pairs={{0,2},{1,3},{2,0},{3,1},{4,6},{5,7},{6,4},{7,5},{8,10},{9,11},{10,... | collective-permute-start | bytes 270344 | tf_op jit(solution)/shard_map/ppermute | solution.py:22
  14.0 9.4 %collective-permute-start.9 = (bf16[2,11,2048]{2,1,0:T(8,128)(2,1)S(1)}, bf16[2,11,2048]{2,1,0:T(8,128)(2,1)S(1)}, u32[]{:S(2)}, u32[]{:S(2)}) collective-permute-start(bf16[2,11,2048]{2,1,0:T(8,128)(2,1)S(1)} %pad_maximum_fusion.5), channel_id=1, source_target_pairs={{0,1},{1,2},{2,3},{3,0},{4,5},{5,6},{6,7},{7,4},{8,9},{9,10},{10,1... | collective-permute-start | bytes 270344 | tf_op jit(solution)/shard_map/ppermute | solution.py:22
  28.9 3.0 %collective-permute-start = (f32[2056,128]{1,0:T(8,128)}, f32[2056,128]{1,0:T(8,128)S(1)}, u32[]{:S(2)}, u32[]{:S(2)}) collective-permute-start(f32[2056,128]{1,0:T(8,128)} %select_maximum_fusion), channel_id=1, source_target_pairs={{0,4},{4,0},{1,5},{5,1},{2,6},{6,2},{3,7},{7,3},{8,12},{12,8},{9,1... | collective-permute-start | bytes 3158024 | tf_op jit(solution)/shard_map/ppermute | solution.py:17
  31.9 108.3 %copy-start.13 = (f32[1,32]{1,0:T(1,128)}, f32[1,32]{1,0:T(1,128)S(1)}, u32[]{:S(2)}) copy-start(f32[1,32]{1,0:T(1,128)S(1)} %get-tuple-element.29) | copy-start | bytes 388
  32.3 109.0 %slice-start = ((f32[1,15,32,256]{3,2,1,0:T(8,128)}), f32[1,9,32,256]{3,2,1,0:T(8,128)S(1)}, s32[]{:S(2)}) async-start(f32[1,15,32,256]{3,2,1,0:T(8,128)} %param.14), calls=%async_computation.1 | async-start | bytes 589824 | tf_op jit(solution)/shard_map/slice | solution.py:137
  33.0 107.1 %collective-permute-start.1 = (bf16[1032,128]{1,0:T(8,128)(2,1)}, bf16[1032,128]{1,0:T(8,128)(2,1)S(1)}, u32[]{:S(2)}, u32[]{:S(2)}) collective-permute-start(bf16[1032,128]{1,0:T(8,128)(2,1)} %fusion.59), channel_id=1, source_target_pairs={{0,8},{8,0},{16,24},{24,16},{32,40},{40,32},{48,56},{56,48},{1,9},... | collective-permute-start | bytes 792584 | tf_op jit(solution)/shard_map/ppermute | solution.py:17
  139.1 76.6 %collective-permute-start.12 = (bf16[2816,2048]{1,0:T(8,128)(2,1)}, bf16[2816,2048]{1,0:T(8,128)(2,1)}, u32[]{:S(2)}, u32[]{:S(2)}) collective-permute-start(bf16[2816,2048]{1,0:T(8,128)(2,1)} %all-gather.2.cloned.1.call-done), channel_id=1, source_target_pairs={{0,4},{4,0},{1,5},{5,1},{2,6},{6,2},{3,7},{7,3},{8,12},{12,8},{9,1... | collective-permute-start | bytes 34603016 | tf_op jit(solution)/shard_map/ppermute | solution.py:17
  140.2 15.0 %copy-start.18 = (f32[1,32]{1,0:T(1,128)}, f32[1,32]{1,0:T(1,128)S(1)}, u32[]{:S(2)}) copy-start(f32[1,32]{1,0:T(1,128)S(1)} %get-tuple-element.23) | copy-start | bytes 388
  140.5 14.7 %copy-start.14 = (f32[1,32]{1,0:T(1,128)S(1)}, f32[1,32]{1,0:T(1,128)}, u32[]{:S(2)}) copy-start(f32[1,32]{1,0:T(1,128)} %copy-done.13) | copy-start | bytes 388
  140.5 14.6 %collective-permute-start.2 = (bf16[1032,128]{1,0:T(8,128)(2,1)S(1)}, bf16[1032,128]{1,0:T(8,128)(2,1)S(1)}, u32[]{:S(2)}, u32[]{:S(2)}) collective-permute-start(bf16[1032,128]{1,0:T(8,128)(2,1)S(1)} %fusion.60), channel_id=1, source_target_pairs={{0,16},{8,24},{16,0},{24,8},{32,48},{40,56},{48,32},{56,40},{1,17}... | collective-permute-start | bytes 792584 | tf_op jit(solution)/shard_map/ppermute | solution.py:17
  143.8 15.0 %copy-start.10 = (f32[256,256]{1,0:T(8,128)S(1)}, f32[256,256]{1,0:T(8,128)}, u32[]{:S(2)}) copy-start(f32[256,256]{1,0:T(8,128)} %fusion.73) | copy-start | bytes 786436
  155.2 18.3 %copy-start.16 = (f32[1,32]{1,0:T(1,128)}, f32[1,32]{1,0:T(1,128)S(1)}, u32[]{:S(2)}) copy-start(f32[1,32]{1,0:T(1,128)S(1)} %get-tuple-element.19) | copy-start | bytes 388
  155.2 18.3 %copy-start.20 = (f32[32]{0:T(128)}, f32[32]{0:T(128)S(1)}, u32[]{:S(2)}) copy-start(f32[32]{0:T(128)S(1)} %get-tuple-element.18) | copy-start | bytes 388
  155.7 17.8 %collective-permute-start.3 = (bf16[1032,128]{1,0:T(8,128)(2,1)S(1)}, bf16[1032,128]{1,0:T(8,128)(2,1)S(1)}, u32[]{:S(2)}, u32[]{:S(2)}) collective-permute-start(bf16[1032,128]{1,0:T(8,128)(2,1)S(1)} %fusion.61), channel_id=1, source_target_pairs={{0,32},{8,40},{16,48},{24,56},{32,0},{40,8},{48,16},{56,24},{1,33}... | collective-permute-start | bytes 792584 | tf_op jit(solution)/shard_map/ppermute | solution.py:17
  173.6 5.9 %copy-start.26 = (f32[1,32]{1,0:T(1,128)}, f32[1,32]{1,0:T(1,128)S(1)}, u32[]{:S(2)}) copy-start(f32[1,32]{1,0:T(1,128)S(1)} %get-tuple-element.14) | copy-start | bytes 388
  174.5 11.4 %collective-permute-start.5 = (bf16[1032,128]{1,0:T(8,128)(2,1)}, bf16[1032,128]{1,0:T(8,128)(2,1)}, u32[]{:S(2)}, u32[]{:S(2)}) collective-permute-start(bf16[1032,128]{1,0:T(8,128)(2,1)} %fusion.62), channel_id=1, source_target_pairs={{0,64},{64,0},{128,192},{192,128},{1,65},{65,1},{129,193},{193,129... | collective-permute-start | bytes 792584 | tf_op jit(solution)/shard_map/ppermute | solution.py:17
  185.2 14.3 %collective-permute-start.4 = (bf16[3,16,64,128]{3,2,1,0:T(8,128)(2,1)}, bf16[3,16,64,128]{3,2,1,0:T(8,128)(2,1)}, u32[]{:S(2)}, u32[]{:S(2)}) collective-permute-start(bf16[3,16,64,128]{3,2,1,0:T(8,128)(2,1)} %pad_maximum_fusion), channel_id=1, source_target_pairs={{0,4},{4,0},{1,5},{5,1},{2,6},{6,2},{3,7},{7,3},{8,12},{12,8},{9,1... | collective-permute-start | bytes 2359304 | tf_op jit(solution)/shard_map/ppermute | solution.py:17
  188.7 9.6 %collective-permute-start.6 = (bf16[1032,128]{1,0:T(8,128)(2,1)S(1)}, bf16[1032,128]{1,0:T(8,128)(2,1)S(1)}, u32[]{:S(2)}, u32[]{:S(2)}) collective-permute-start(bf16[1032,128]{1,0:T(8,128)(2,1)S(1)} %fusion.63), channel_id=1, source_target_pairs={{0,128},{64,192},{128,0},{192,64},{1,129},{65,193},{129,1},{193,65... | collective-permute-start | bytes 792584 | tf_op jit(solution)/shard_map/ppermute | solution.py:17
  198.4 3.7 %collective-permute-start.7 = (bf16[2,16,64,128]{3,2,1,0:T(8,128)(2,1)S(1)}, bf16[2,16,64,128]{3,2,1,0:T(8,128)(2,1)S(1)}, u32[]{:S(2)}, u32[]{:S(2)}) collective-permute-start(bf16[2,16,64,128]{3,2,1,0:T(8,128)(2,1)S(1)} %pad_maximum_fusion.3), channel_id=1, source_target_pairs={{0,4},{4,0},{1,5},{5,1},{2,6},{6,2},{3,7},{7,3},{8,12},{12,8},{9,1... | collective-permute-start | bytes 1572872 | tf_op jit(solution)/shard_map/ppermute | solution.py:17
  215.7 9.6 %copy-start.1 = (bf16[1,256,128]{2,1,0:T(8,128)(2,1)S(1)}, bf16[1,256,128]{2,1,0:T(8,128)(2,1)}, u32[]{:S(2)}) copy-start(bf16[1,256,128]{2,1,0:T(8,128)(2,1)} %param.12) | copy-start | bytes 196612
  (20 other events, 59.3 us)
Sparse Core Ops, SparseCore 0:
  24.7 114.3 all-gather.1

commit v2 on v1

--- a/solution.py
+++ b/solution.py
@@ -87,7 +87,6 @@
     core = lax.axis_index("core")
     here = (lax.axis_index("x") * lax.axis_size("z") + lax.axis_index("z")) * 2 + core
     mine = gathered_weights(w_gate, w_up, core, lax.axis_index("dp"))
-    other = swapped(mine, "core", 1)
 
     x_blk = x_in[0].reshape(tokens, heads, head_dim)
     b_blk, c_blk = keys_b[0], queries_c[0]
@@ -145,9 +144,12 @@
     normed = (
         gated * lax.rsqrt(jnp.mean(gated * gated, axis=-1, keepdims=True) + EPS) * norm_gain
     ).astype(jnp.bfloat16)
+    normed = lax.optimization_barrier(normed)
     dims = (((1,), (1,)), ((), ()))
+    theirs = swapped(normed, "core", 1)
+    sent = lax.dot_general(theirs, mine, dims, preferred_element_type=jnp.float32)
+    other_part = swapped(sent, "core", 1)
     own_part = lax.dot_general(normed, mine, dims, preferred_element_type=jnp.float32)
-    other_part = lax.dot_general(normed, other, dims, preferred_element_type=jnp.float32)
     gate_pre = jnp.where(core == 0, own_part, other_part)
     up_pre = jnp.where(core == 0, other_part, own_part)
     return (jax.nn.silu(gate_pre) * up_pre).astype(jnp.bfloat16)[None]

time: 233 us -> 180 us (0.77)
  waiting for transfers between devices: 140 us -> 78.4 us
  starting transfers between devices: 16 us -> 25.7 us
  matrix products: 36.4 us -> 32.6 us
    all_gather x1, waiting for transfers between devices: 103 us -> 28.3 us  [gathered_weights(): return lax.all_gather(block, ('x', 'z'), axis=0, tiled=True)]
    ppermute x10 -> x11, waiting for transfers between devices: 28.2 us -> 43.4 us  [swapped(): lax.ppermute(value, axis, [(i, i ^ mask) for i in range(lax.axis_size(axi...]
    ppermute x10 -> x11, starting transfers between devices: 13.8 us -> 22.9 us  [swapped(): lax.ppermute(value, axis, [(i, i ^ mask) for i in range(lax.axis_size(axi...]
    dot_general x1, matrix products: 9.6 us -> 6.31 us  [per_device(): lax.dot_general(theirs, mine, dims, preferred_element_type=jnp.float32)]
    unnamed x60 -> x58, local copies, waits for them, and re-layouts: 4.32 us -> 5.8 us
  transfers between devices with their start and end apart: 14 -> 15, of which waited for: 9 -> 11; matrix products, arithmetic and copies ran while one was open for 21% -> 27% of each run, Pallas kernels for 0% -> 0%
where the time goes in v2:
time: 180 us
  waiting for transfers between devices  78.4 us (44%)
  matrix products  32.6 us (18%)
  starting transfers between devices  25.7 us (14%)
  local copies, waits for them, and re-layouts  15.7 us (9%)
  between operations  14 us (8%)
  other arithmetic  13.4 us (7%)
    ppermute x11, waiting for transfers between devices, swapped(): lax.ppermute(value, axis, [(i, i ^ mask) for i in range(lax.axis_size(axi...  43.4 us
    all_gather x1, waiting for transfers between devices, gathered_weights(): return lax.all_gather(block, ('x', 'z'), axis=0, tiled=True)  28.3 us
    ppermute x11, starting transfers between devices, swapped(): lax.ppermute(value, axis, [(i, i ^ mask) for i in range(lax.axis_size(axi...  22.9 us
    dot_general x1, matrix products, local_mix(): chosen = jnp.einsum('lht,lts->hts', mix_low, level_picks, precision=HIGH)  7.5 us
    ppermute x3, waiting for transfers between devices, shifted(): lax.ppermute(value, axis, [(i, (i + step) % count) for i in range(count)])  6.62 us
    dot_general x1, matrix products, per_device(): lax.dot_general(normed, mine, dims, preferred_element_type=jnp.float32)  6.34 us
    dot_general x1, matrix products, per_device(): lax.dot_general(theirs, mine, dims, preferred_element_type=jnp.float32)  6.31 us
    unnamed x58, local copies, waits for them, and re-layouts  5.8 us
  transfers between devices with their start and end apart: 15, of which 11 were waited for; matrix products, arithmetic and copies ran while one was open for 27% of the time, Pallas kernels for 0%

profile of v2, /device:TPU:1, one launch (start us, length us, event | category | flops | bytes accessed | tf_op | source)
XLA Modules:
  0.0 179.7 jit_solution(6422862122470889307)
XLA Ops:
  7.4 3.3 %collective-permute-start.8 = (bf16[11,2048]{1,0:T(8,128)(2,1)S(1)}, bf16[11,2048]{1,0:T(8,128)(2,1)S(1)}, u32[]{:S(2)}, u32[]{:S(2)}) collective-permute-start(bf16[11,2048]{1,0:T(8,128)(2,1)S(1)} %select_bitcast_fusion.4), channel_id=1, source_target_pairs={{0,4},{4,0},{1,5},{5,1},{2,6},{6,2},{3,7},{7,3},{8,12},{12,8},{9,1... | collective-permute-start | bytes 135176 | tf_op jit(solution)/shard_map/ppermute | solution.py:17
  15.3 3.6 %collective-permute-done.10 = bf16[2,11,2048]{2,1,0:T(8,128)(2,1)S(1)} collective-permute-done((bf16[2,11,2048]{2,1,0:T(8,128)(2,1)S(1)}, bf16[2,11,2048]{2,1,0:T(8,128)(2,1)S(1)}, u32[]{:S(2)}, u32[]{:S(2)}) %collective-permute-start.10) | collective-permute-done | bytes 90144 | tf_op jit(solution)/shard_map/ppermute | solution.py:22
  20.3 1.6 collective-permute-done.9
  33.5 5.9 %collective-permute-done.1 = bf16[1032,128]{1,0:T(8,128)(2,1)S(1)} collective-permute-done((bf16[1032,128]{1,0:T(8,128)(2,1)S(1)}, bf16[1032,128]{1,0:T(8,128)(2,1)S(1)}, u32[]{:S(2)}, u32[]{:S(2)}) %collective-permute-start.1) | collective-permute-done | bytes 264224 | tf_op jit(solution)/shard_map/ppermute | solution.py:17
  39.7 2.3 %collective-permute-start.2 = (bf16[1032,128]{1,0:T(8,128)(2,1)S(1)}, bf16[1032,128]{1,0:T(8,128)(2,1)S(1)}, u32[]{:S(2)}, u32[]{:S(2)}) collective-permute-start(bf16[1032,128]{1,0:T(8,128)(2,1)S(1)} %fusion.60), channel_id=1, source_target_pairs={{0,16},{8,24},{16,0},{24,8},{32,48},{40,56},{48,32},{56,40},{1,17}... | collective-permute-start | bytes 792584 | tf_op jit(solution)/shard_map/ppermute | solution.py:17
  42.2 2.5 %copy.30 = f32[1,9,32,256]{2,1,3,0:T(8,128)} copy(f32[1,9,32,256]{3,2,1,0:T(8,128)S(1)} %slice-done) | data formatting | bytes 589824
  44.7 12.7 %collective-permute-done.2 = bf16[1032,128]{1,0:T(8,128)(2,1)S(1)} collective-permute-done((bf16[1032,128]{1,0:T(8,128)(2,1)S(1)}, bf16[1032,128]{1,0:T(8,128)(2,1)S(1)}, u32[]{:S(2)}, u32[]{:S(2)}) %collective-permute-start.2) | collective-permute-done | bytes 264224 | tf_op jit(solution)/shard_map/ppermute | solution.py:17
  57.9 7.5 %collective-permute-start.3 = (bf16[1032,128]{1,0:T(8,128)(2,1)S(1)}, bf16[1032,128]{1,0:T(8,128)(2,1)S(1)}, u32[]{:S(2)}, u32[]{:S(2)}) collective-permute-start(bf16[1032,128]{1,0:T(8,128)(2,1)S(1)} %fusion.61), channel_id=1, source_target_pairs={{0,32},{8,40},{16,48},{24,56},{32,0},{40,8},{48,16},{56,24},{1,33}... | collective-permute-start | bytes 792584 | tf_op jit(solution)/shard_map/ppermute | solution.py:17
  65.5 7.5 %fusion.1 = bf16[32,256,256]{2,0,1:T(8,128)(2,1)} fusion(f32[256,256]{1,0:T(8,128)S(1)} %copy-done.12, f32[32,256]{1,0:T(8,128)S(1)} %copy_bitcast_fusion, f32[32,256]{0,1:T(8,128)S(1)} %copy.24, pred[256,256]{1,0:T(8,128)(4,1)S(1)} %iota_compare_fusion.6, f32[1,9,32,256]{2,1,3,0:T(8,128)S(1)} %copy-done.6, s32[256,256]{1,0:T(8,128)S(1)} %add_select_fusion), kind=kOutput, calls=%fused_computation.2 | convolution fusion | flops 237568000 | bytes 5144576 | tf_op jit(solution)/shard_map/lht,lts->hts/dot_general | solution.py:39
  73.0 7.3 %collective-permute-done.3 = bf16[1032,128]{1,0:T(8,128)(2,1)S(1)} collective-permute-done((bf16[1032,128]{1,0:T(8,128)(2,1)S(1)}, bf16[1032,128]{1,0:T(8,128)(2,1)S(1)}, u32[]{:S(2)}, u32[]{:S(2)}) %collective-permute-start.3) | collective-permute-done | bytes 264224 | tf_op jit(solution)/shard_map/ppermute | solution.py:17
  81.3 2.0 %collective-permute-start.5 = (bf16[1032,128]{1,0:T(8,128)(2,1)}, bf16[1032,128]{1,0:T(8,128)(2,1)}, u32[]{:S(2)}, u32[]{:S(2)}) collective-permute-start(bf16[1032,128]{1,0:T(8,128)(2,1)} %fusion.62), channel_id=1, source_target_pairs={{0,64},{64,0},{128,192},{192,128},{1,65},{65,1},{129,193},{193,129... | collective-permute-start | bytes 792584 | tf_op jit(solution)/shard_map/ppermute | solution.py:17
  83.2 5.0 %fusion.2 = f32[32,256,64]{1,2,0:T(8,128)S(1)} fusion(bf16[256,32,64]{0,2,1:T(8,128)(2,1)} %bitcast.279, bf16[32,256,256]{2,0,1:T(8,128)(2,1)} %fusion.1), kind=kOutput, calls=%fused_computation.5 | convolution fusion | flops 268435456 | bytes 7340032 | tf_op jit(solution)/shard_map/hts,shp->thp/dot_general | solution.py:44
  88.3 2.6 %copy.28 = f32[1,256,2048]{1,2,0:T(8,128)} copy(bf16[1,256,2048]{2,1,0:T(8,128)(2,1)} %param.10) | data formatting | bytes 3145728 | tf_op jit(solution)/shard_map/convert_element_type | solution.py:143
  90.9 2.1 %slice.204 = bf16[2048,128]{1,0:T(8,128)(2,1)} slice(f32[2056,128]{1,0:T(8,128)} %copy-done.5), slice={[0:2048], [0:128]} | slice | bytes 1048576 | tf_op jit(solution)/shard_map/slice | solution.py:61
  94.0 1.8 collective-permute-start.4
  98.6 2.3 %collective-permute-start.6 = (bf16[1032,128]{1,0:T(8,128)(2,1)S(1)}, bf16[1032,128]{1,0:T(8,128)(2,1)S(1)}, u32[]{:S(2)}, u32[]{:S(2)}) collective-permute-start(bf16[1032,128]{1,0:T(8,128)(2,1)S(1)} %fusion.63), channel_id=1, source_target_pairs={{0,128},{64,192},{128,0},{192,64},{1,129},{65,193},{129,1},{193,65... | collective-permute-start | bytes 792584 | tf_op jit(solution)/shard_map/ppermute | solution.py:17
  101.5 12.5 %collective-permute-done.6 = bf16[1032,128]{1,0:T(8,128)(2,1)S(1)} collective-permute-done((bf16[1032,128]{1,0:T(8,128)(2,1)S(1)}, bf16[1032,128]{1,0:T(8,128)(2,1)S(1)}, u32[]{:S(2)}, u32[]{:S(2)}) %collective-permute-start.6) | collective-permute-done | bytes 264224 | tf_op jit(solution)/shard_map/ppermute | solution.py:17
  119.3 3.0 %multiply_reduce_fusion = (f32[256]{0:T(256)S(1)}, f32[256,32,64]{0,2,1:T(8,128)}) fusion(f32[256,32,64]{0,2,1:T(8,128)S(1)} %bitcast.268, bf16[1,256,128]{2,1,0:T(8,128)(2,1)S(1)} %copy-done, bf16[2,16,64,128]{3,2,1,0:T(8,128)(2,1)S(1)} %get-tuple-element.34, bf16[2,16,64,128]{3,2,1,0:T(8,128)(2,1)S(1)} %get-tuple-element.35, ...), kind=kOutput, calls=%fused_computation.33 | convolution fusion | flops 144441088 | bytes 18088960 | tf_op jit(solution)/shard_map/tn,hpn->thp/dot_general | solution.py:140
  122.2 2.0 %copy.27 = f32[256,2048]{1,0:T(8,128)S(1)} copy(f32[256,2048]{0,1:T(8,128)} %bitcast.269) | data formatting | bytes 4194304 | tf_op jit(solution)/shard_map/reshape | solution.py:142
  126.2 2.5 %collective-permute-done.12 = bf16[256,2048]{1,0:T(8,128)(2,1)S(1)} collective-permute-done((bf16[256,2048]{1,0:T(8,128)(2,1)S(1)}, bf16[256,2048]{1,0:T(8,128)(2,1)S(1)}, u32[]{:S(2)}, u32[]{:S(2)}) %collective-permute-start.12) | collective-permute-done | bytes 1048608 | tf_op jit(solution)/shard_map/ppermute | solution.py:17
  128.8 28.3 %all-gather.2.cloned.1.call-done = bf16[2816,2048]{1,0:T(8,128)(2,1)} async-done(((bf16[88,2048]{1,0:T(8,128)(2,1)}), bf16[2816,2048]{1,0:T(8,128)(2,1)}) %all-gather.2.cloned.1.call-update) | async-done | bytes 11534352 | tf_op jit(solution)/shard_map/all_gather | solution.py:79
  157.1 6.3 %fusion.107 = f32[256,2816]{1,0:T(8,128)S(1)} fusion(bf16[256,2048]{1,0:T(8,128)(2,1)S(1)} %collective-permute-done.12, bf16[2816,2048]{1,0:T(8,128)(2,1)} %all-gather.2.cloned.1.call-done), kind=kOutput, calls=%fused_computation.218 | convolution fusion | flops 2952790016 | bytes 15466496 | tf_op jit(solution)/shard_map/dot_general | solution.py:150
  164.5 6.3 %fusion.106 = f32[256,2816]{1,0:T(8,128)S(1)} fusion(bf16[256,2048]{1,0:T(8,128)(2,1)S(1)} %copy-done.10, bf16[2816,2048]{1,0:T(8,128)(2,1)} %all-gather.2.cloned.1.call-done), kind=kOutput, calls=%fused_computation.217 | convolution fusion | flops 2952790016 | bytes 15466496 | tf_op jit(solution)/shard_map/dot_general | solution.py:152
  170.9 1.9 %fusion.23 = bf16[1,256,2816]{2,1,0:T(8,128)(2,1)} fusion(f32[256,2816]{1,0:T(8,128)S(1)} %collective-permute-done.13, f32[256,2816]{1,0:T(8,128)S(1)} %fusion.106, pred[]{:T(512)S(6)} %eq.88), kind=kLoop, calls=%fused_computation.42 | loop fusion | flops 5767168 | bytes 7208961 | tf_op jit(solution)/shard_map/broadcast_in_dim | solution.py:155
  (166 shorter events, 32.7 us)
Async XLA Ops:
  6.5 21.9 %copy-start = (bf16[1,256,128]{2,1,0:T(8,128)(2,1)S(1)}, bf16[1,256,128]{2,1,0:T(8,128)(2,1)}, u32[]{:S(2)}) copy-start(bf16[1,256,128]{2,1,0:T(8,128)(2,1)} %param.12) | copy-start | bytes 196612
  6.5 150.6 %all-gather.2.cloned.1.call-start = ((), (), s32[]{:S(2)}) async-start(), calls=%async_computation | async-start | bytes 11894784 | tf_op jit(solution)/shard_map/all_gather | solution.py:79
  7.4 4.2 %collective-permute-start.8 = (bf16[11,2048]{1,0:T(8,128)(2,1)S(1)}, bf16[11,2048]{1,0:T(8,128)(2,1)S(1)}, u32[]{:S(2)}, u32[]{:S(2)}) collective-permute-start(bf16[11,2048]{1,0:T(8,128)(2,1)S(1)} %select_bitcast_fusion.4), channel_id=1, source_target_pairs={{0,4},{4,0},{1,5},{5,1},{2,6},{6,2},{3,7},{7,3},{8,12},{12,8},{9,1... | collective-permute-start | bytes 135176 | tf_op jit(solution)/shard_map/ppermute | solution.py:17
  12.5 6.3 %collective-permute-start.10 = (bf16[2,11,2048]{2,1,0:T(8,128)(2,1)S(1)}, bf16[2,11,2048]{2,1,0:T(8,128)(2,1)S(1)}, u32[]{:S(2)}, u32[]{:S(2)}) collective-permute-start(bf16[2,11,2048]{2,1,0:T(8,128)(2,1)S(1)} %pad_maximum_fusion.5), channel_id=1, source_target_pairs={{0,2},{1,3},{2,0},{3,1},{4,6},{5,7},{6,4},{7,5},{8,10},{9,11},{10,... | collective-permute-start | bytes 270344 | tf_op jit(solution)/shard_map/ppermute | solution.py:22
  13.8 6.5 %collective-permute-start.11 = (bf16[2,11,2048]{2,1,0:T(8,128)(2,1)S(1)}, bf16[2,11,2048]{2,1,0:T(8,128)(2,1)S(1)}, u32[]{:S(2)}, u32[]{:S(2)}) collective-permute-start(bf16[2,11,2048]{2,1,0:T(8,128)(2,1)S(1)} %pad_maximum_fusion.5), channel_id=1, source_target_pairs={{0,3},{1,0},{2,1},{3,2},{4,7},{5,4},{6,5},{7,6},{8,11},{9,8},{10,9... | collective-permute-start | bytes 270344 | tf_op jit(solution)/shard_map/ppermute | solution.py:22
  14.6 7.3 %collective-permute-start.9 = (bf16[2,11,2048]{2,1,0:T(8,128)(2,1)S(1)}, bf16[2,11,2048]{2,1,0:T(8,128)(2,1)S(1)}, u32[]{:S(2)}, u32[]{:S(2)}) collective-permute-start(bf16[2,11,2048]{2,1,0:T(8,128)(2,1)S(1)} %pad_maximum_fusion.5), channel_id=1, source_target_pairs={{0,1},{1,2},{2,3},{3,0},{4,5},{5,6},{6,7},{7,4},{8,9},{9,10},{10,1... | collective-permute-start | bytes 270344 | tf_op jit(solution)/shard_map/ppermute | solution.py:22
  27.4 3.5 %collective-permute-start = (f32[2056,128]{1,0:T(8,128)}, f32[2056,128]{1,0:T(8,128)S(1)}, u32[]{:S(2)}, u32[]{:S(2)}) collective-permute-start(f32[2056,128]{1,0:T(8,128)} %select_maximum_fusion), channel_id=1, source_target_pairs={{0,4},{4,0},{1,5},{5,1},{2,6},{6,2},{3,7},{7,3},{8,12},{12,8},{9,1... | collective-permute-start | bytes 3158024 | tf_op jit(solution)/shard_map/ppermute | solution.py:17
  31.3 10.9 %slice-start = ((f32[1,15,32,256]{3,2,1,0:T(8,128)}), f32[1,9,32,256]{3,2,1,0:T(8,128)S(1)}, s32[]{:S(2)}) async-start(f32[1,15,32,256]{3,2,1,0:T(8,128)} %param.14), calls=%async_computation.1 | async-start | bytes 589824 | tf_op jit(solution)/shard_map/slice | solution.py:136
  31.8 7.6 %collective-permute-start.1 = (bf16[1032,128]{1,0:T(8,128)(2,1)S(1)}, bf16[1032,128]{1,0:T(8,128)(2,1)S(1)}, u32[]{:S(2)}, u32[]{:S(2)}) collective-permute-start(bf16[1032,128]{1,0:T(8,128)(2,1)S(1)} %fusion.59), channel_id=1, source_target_pairs={{0,8},{8,0},{16,24},{24,16},{32,40},{40,32},{48,56},{56,48},{1,9},... | collective-permute-start | bytes 792584 | tf_op jit(solution)/shard_map/ppermute | solution.py:17
  39.4 18.0 %copy-start.18 = (f32[1,32]{1,0:T(1,128)}, f32[1,32]{1,0:T(1,128)S(1)}, u32[]{:S(2)}) copy-start(f32[1,32]{1,0:T(1,128)S(1)} %get-tuple-element.23) | copy-start | bytes 388
  39.7 17.7 %collective-permute-start.2 = (bf16[1032,128]{1,0:T(8,128)(2,1)S(1)}, bf16[1032,128]{1,0:T(8,128)(2,1)S(1)}, u32[]{:S(2)}, u32[]{:S(2)}) collective-permute-start(bf16[1032,128]{1,0:T(8,128)(2,1)S(1)} %fusion.60), channel_id=1, source_target_pairs={{0,16},{8,24},{16,0},{24,8},{32,48},{40,56},{48,32},{56,40},{1,17}... | collective-permute-start | bytes 792584 | tf_op jit(solution)/shard_map/ppermute | solution.py:17
  44.7 20.8 %copy-start.12 = (f32[256,256]{1,0:T(8,128)S(1)}, f32[256,256]{1,0:T(8,128)}, u32[]{:S(2)}) copy-start(f32[256,256]{1,0:T(8,128)} %fusion.73) | copy-start | bytes 786436
  57.4 22.8 %copy-start.15 = (f32[1,32]{1,0:T(1,128)}, f32[1,32]{1,0:T(1,128)S(1)}, u32[]{:S(2)}) copy-start(f32[1,32]{1,0:T(1,128)S(1)} %get-tuple-element.19) | copy-start | bytes 388
  57.4 22.8 %copy-start.20 = (f32[32]{0:T(128)}, f32[32]{0:T(128)S(1)}, u32[]{:S(2)}) copy-start(f32[32]{0:T(128)S(1)} %get-tuple-element.18) | copy-start | bytes 388
  57.6 7.9 %copy-start.6 = (f32[1,9,32,256]{2,1,3,0:T(8,128)S(1)}, f32[1,9,32,256]{2,1,3,0:T(8,128)}, u32[]{:S(2)}) copy-start(f32[1,9,32,256]{2,1,3,0:T(8,128)} %copy.30) | copy-start | bytes 884740
  57.9 22.3 %collective-permute-start.3 = (bf16[1032,128]{1,0:T(8,128)(2,1)S(1)}, bf16[1032,128]{1,0:T(8,128)(2,1)S(1)}, u32[]{:S(2)}, u32[]{:S(2)}) collective-permute-start(bf16[1032,128]{1,0:T(8,128)(2,1)S(1)} %fusion.61), channel_id=1, source_target_pairs={{0,32},{8,40},{16,48},{24,56},{32,0},{40,8},{48,16},{56,24},{1,33}... | collective-permute-start | bytes 792584 | tf_op jit(solution)/shard_map/ppermute | solution.py:17
  81.3 14.5 %collective-permute-start.5 = (bf16[1032,128]{1,0:T(8,128)(2,1)}, bf16[1032,128]{1,0:T(8,128)(2,1)}, u32[]{:S(2)}, u32[]{:S(2)}) collective-permute-start(bf16[1032,128]{1,0:T(8,128)(2,1)} %fusion.62), channel_id=1, source_target_pairs={{0,64},{64,0},{128,192},{192,128},{1,65},{65,1},{129,193},{193,129... | collective-permute-start | bytes 792584 | tf_op jit(solution)/shard_map/ppermute | solution.py:17
  94.0 21.1 %collective-permute-start.4 = (bf16[3,16,64,128]{3,2,1,0:T(8,128)(2,1)}, bf16[3,16,64,128]{3,2,1,0:T(8,128)(2,1)}, u32[]{:S(2)}, u32[]{:S(2)}) collective-permute-start(bf16[3,16,64,128]{3,2,1,0:T(8,128)(2,1)} %pad_maximum_fusion), channel_id=1, source_target_pairs={{0,4},{4,0},{1,5},{5,1},{2,6},{6,2},{3,7},{7,3},{8,12},{12,8},{9,1... | collective-permute-start | bytes 2359304 | tf_op jit(solution)/shard_map/ppermute | solution.py:17
  98.6 15.4 %collective-permute-start.6 = (bf16[1032,128]{1,0:T(8,128)(2,1)S(1)}, bf16[1032,128]{1,0:T(8,128)(2,1)S(1)}, u32[]{:S(2)}, u32[]{:S(2)}) collective-permute-start(bf16[1032,128]{1,0:T(8,128)(2,1)S(1)} %fusion.63), channel_id=1, source_target_pairs={{0,128},{64,192},{128,0},{192,64},{1,129},{65,193},{129,1},{193,65... | collective-permute-start | bytes 792584 | tf_op jit(solution)/shard_map/ppermute | solution.py:17
  114.1 3.5 %collective-permute-start.7 = (bf16[2,16,64,128]{3,2,1,0:T(8,128)(2,1)S(1)}, bf16[2,16,64,128]{3,2,1,0:T(8,128)(2,1)S(1)}, u32[]{:S(2)}, u32[]{:S(2)}) collective-permute-start(bf16[2,16,64,128]{3,2,1,0:T(8,128)(2,1)S(1)} %pad_maximum_fusion.3), channel_id=1, source_target_pairs={{0,4},{4,0},{1,5},{5,1},{2,6},{6,2},{3,7},{7,3},{8,12},{12,8},{9,1... | collective-permute-start | bytes 1572872 | tf_op jit(solution)/shard_map/ppermute | solution.py:17
  126.1 2.7 %collective-permute-start.12 = (bf16[256,2048]{1,0:T(8,128)(2,1)S(1)}, bf16[256,2048]{1,0:T(8,128)(2,1)S(1)}, u32[]{:S(2)}, u32[]{:S(2)}) collective-permute-start(bf16[256,2048]{1,0:T(8,128)(2,1)S(1)} %fusion.22), channel_id=1, source_target_pairs={{0,4},{4,0},{1,5},{5,1},{2,6},{6,2},{3,7},{7,3},{8,12},{12,8},{9,1... | collective-permute-start | bytes 3145736 | tf_op jit(solution)/shard_map/ppermute | solution.py:17
  126.2 38.3 %copy-start.10 = (bf16[256,2048]{1,0:T(8,128)(2,1)S(1)}, bf16[256,2048]{1,0:T(8,128)(2,1)}, u32[]{:S(2)}) copy-start(bf16[256,2048]{1,0:T(8,128)(2,1)} %copy-done.9) | copy-start | bytes 3145732
  163.4 7.5 %collective-permute-start.13 = (f32[256,2816]{1,0:T(8,128)S(1)}, f32[256,2816]{1,0:T(8,128)S(1)}, u32[]{:S(2)}, u32[]{:S(2)}) collective-permute-start(f32[256,2816]{1,0:T(8,128)S(1)} %fusion.107), channel_id=1, source_target_pairs={{0,4},{4,0},{1,5},{5,1},{2,6},{6,2},{3,7},{7,3},{8,12},{12,8},{9,1... | collective-permute-start | bytes 8650760 | tf_op jit(solution)/shard_map/ppermute | solution.py:17
  164.5 8.3 %copy-start.1 = (bf16[1,256,128]{2,1,0:T(8,128)(2,1)S(1)}, bf16[1,256,128]{2,1,0:T(8,128)(2,1)}, u32[]{:S(2)}) copy-start(bf16[1,256,128]{2,1,0:T(8,128)(2,1)} %param.12) | copy-start | bytes 196612
  (20 other events, 67.2 us)
Sparse Core Ops, SparseCore 0:
  23.2 133.8 all-gather.1

commit v3 on v2

--- a/solution.py
+++ b/solution.py
@@ -1,6 +1,8 @@
 import jax
 import jax.numpy as jnp
 from jax import lax
+from jax.experimental import pallas as pl
+from jax.experimental.pallas import tpu as pltpu
 from jax.sharding import Mesh
 from jax.sharding import PartitionSpec as P
 
@@ -11,6 +13,7 @@
 SEQ = ("x", "z", "core")
 STEPS = (("z", 1), ("z", 2), ("z", 4), ("x", 1), ("x", 2))
 HEAD_DIM = 64
+DIMS = (((1,), (1,)), ((), ()))
 
 
 def swapped(value, axis, mask):
@@ -79,6 +82,69 @@
     return lax.all_gather(block, ("x", "z"), axis=0, tiled=True)
 
 
+def mix_kernel(local, first, near, far, c_blk, scales, gate_in, gain, out, gated, squares):
+    step = pl.program_id(0)
+    width = local.shape[1]
+    heads = scales.shape[2]
+    head = lax.broadcasted_iota(jnp.int32, (2 * heads, width), 0) & (heads - 1)
+    lane = lax.broadcasted_iota(jnp.int32, (2 * heads, width), 1) + step * width
+    spread = (head == lane >> 6).astype(jnp.float32).astype(jnp.bfloat16)
+    levels = [first[...]] + [near[k] for k in range(3)] + [far[k] for k in range(2)]
+    mixed = local[...]
+    for rank, level in enumerate(levels):
+        scale = scales[rank]
+        top = scale.astype(jnp.bfloat16)
+        low = (scale - top.astype(jnp.float32)).astype(jnp.bfloat16)
+        both = jnp.concatenate([top, low], axis=1)
+        wide = jnp.dot(both, spread, preferred_element_type=jnp.float32)
+        product = lax.dot_general(c_blk[...], level, DIMS, preferred_element_type=jnp.float32)
+        mixed = mixed + wide * product
+    value = mixed * jax.nn.silu(gate_in[...].astype(jnp.float32))
+    gated[:, pl.ds(pl.multiple_of(step * width, width), width)] = value
+    part = jnp.sum(value * value, axis=1, keepdims=True)
+
+    @pl.when(step == 0)
+    def _():
+        squares[...] = part
+
+    @pl.when(step > 0)
+    def _():
+        squares[...] += part
+
+    @pl.when(step == pl.num_programs(0) - 1)
+    def _():
+        rate = lax.rsqrt(squares[...] * (1.0 / out.shape[1]) + EPS)
+        out[...] = (gated[...] * rate * gain[...]).astype(out.dtype)
+
+
+def mixed_and_normed(local, first, near, far, c_blk, scales, gate_in, gain):
+    tokens, width = local.shape
+    size = c_blk.shape[1]
+    cut = 256
+    column = pl.BlockSpec((tokens, cut), lambda j: (0, j))
+    return pl.pallas_call(
+        mix_kernel,
+        grid=(width // cut,),
+        in_specs=[
+            column,
+            pl.BlockSpec((cut, size), lambda j: (j, 0)),
+            pl.BlockSpec((3, cut, size), lambda j: (0, j, 0)),
+            pl.BlockSpec((2, cut, size), lambda j: (0, j, 0)),
+            pl.BlockSpec(c_blk.shape, lambda j: (0, 0)),
+            pl.BlockSpec(scales.shape, lambda j: (0, 0, 0)),
+            column,
+            pl.BlockSpec((1, width), lambda j: (0, 0)),
+        ],
+        out_specs=pl.BlockSpec((tokens, width), lambda j: (0, 0)),
+        out_shape=jax.ShapeDtypeStruct((tokens, width), jnp.bfloat16),
+        scratch_shapes=[pltpu.VMEM((tokens, width), jnp.float32), pltpu.VMEM((tokens, 1), jnp.float32)],
+        compiler_params=pltpu.CompilerParams(vmem_limit_bytes=32 * 2**20),
+        cost_estimate=pl.CostEstimate(
+            flops=14 * tokens * width * size, bytes_accessed=8 * 2**20, transcendentals=tokens * width
+        ),
+    )(local, first, near, far, c_blk, scales, gate_in, gain)
+
+
 def per_device(x_in, gate_in, keys_b, queries_c, decay_log, level_mix, norm_gain, w_gate, w_up):
     tokens, width = x_in.shape[1:]
     heads = decay_log.shape[1]
@@ -110,6 +176,9 @@
     upper, lead = [core == 1], [prefix]
     prefix = jnp.where(core == 1, their_decay, 0.0)
     levels = []
+    start = core * half
+    quarter = half // 2
+    odd = lax.axis_index("z") & 1
     for bit, (axis, mask) in enumerate(STEPS, 1):
         received = swapped(packed(summary, total, jnp.bfloat16), axis, mask)
         levels.append(received[:-8])
@@ -117,41 +186,52 @@
         is_upper = here >> bit & 1 == 1
         upper.append(is_upper)
         lead.append(prefix)
+        if bit == 1:
+            summary = lax.dynamic_slice_in_dim(summary, odd * quarter, quarter)
+            their_state = lax.dynamic_slice_in_dim(their_state, odd * quarter, quarter)
+            start = start + odd * quarter
         if bit < len(STEPS):
             lower_state = jnp.where(is_upper, their_state, summary)
             upper_state = jnp.where(is_upper, summary, their_state)
             upper_decay = jnp.where(is_upper, total, their_decay)
-            gain = lax.dynamic_slice_in_dim(jnp.exp(upper_decay), core * half, half)
+            gain = lax.dynamic_slice_in_dim(jnp.exp(upper_decay), start, quarter)
             summary = gain[:, None, None] * lower_state + upper_state
             prefix = jnp.where(is_upper, prefix + their_decay, prefix)
             total = total + their_decay
 
-    def whole(own):
-        own = jnp.stack(own).reshape(len(own), half, head_dim, -1)
-        theirs = swapped(own, "core", 1)
-        pair = (jnp.where(core == 0, own, theirs), jnp.where(core == 0, theirs, own))
-        return list(jnp.concatenate(pair, axis=1))
-
-    all_levels = [first_level] + whole(levels[:3]) + whole(levels[3:])
-    mixed = local_mix(x_blk, b_blk, c_blk, running, mix[:inner])
-    for rank, level in enumerate(all_levels):
+    def joined(own, axis, place):
+        theirs = swapped(own, axis, 1)
+        pair = (jnp.where(place == 0, own, theirs), jnp.where(place == 0, theirs, own))
+        return jnp.concatenate(pair, axis=1)
+
+    def split(rows):
+        return rows.reshape(1, -1, head_dim, rows.shape[1])
+
+    near = joined(jnp.concatenate([split(levels[1]), split(levels[2])]), "z", odd)
+    near = joined(jnp.concatenate([split(levels[0]), near]), "core", core)
+    far = joined(jnp.concatenate([split(levels[3]), split(levels[4])]), "z", odd)
+    far = joined(far, "core", core)
+    local = local_mix(x_blk, b_blk, c_blk, running, mix[:inner] + levels[0][:1, :1] * 0)
+    scales = []
+    for rank in range(mix.shape[0] - inner):
         growth = jnp.where(upper[rank], jnp.exp(running + lead[rank][:, None]), 0.0)
-        scale = (mix[inner + rank] * growth).T
-        product = jnp.einsum("tn,hpn->thp", c_blk, level, preferred_element_type=jnp.float32)
-        mixed = mixed + scale[:, :, None] * product
-    mixed = mixed.reshape(tokens, width)
-    gated = mixed * jax.nn.silu(gate_in[0].astype(jnp.float32))
-    normed = (
-        gated * lax.rsqrt(jnp.mean(gated * gated, axis=-1, keepdims=True) + EPS) * norm_gain
-    ).astype(jnp.bfloat16)
-    normed = lax.optimization_barrier(normed)
-    dims = (((1,), (1,)), ((), ()))
+        scales.append((mix[inner + rank] * growth).T)
+    normed = mixed_and_normed(
+        local.reshape(tokens, width),
+        first_level.reshape(width, -1),
+        near.reshape(3, width, -1),
+        far.reshape(2, width, -1),
+        c_blk,
+        jnp.stack(scales),
+        gate_in[0],
+        norm_gain[None],
+    )
     theirs = swapped(normed, "core", 1)
-    sent = lax.dot_general(theirs, mine, dims, preferred_element_type=jnp.float32)
-    other_part = swapped(sent, "core", 1)
-    own_part = lax.dot_general(normed, mine, dims, preferred_element_type=jnp.float32)
-    gate_pre = jnp.where(core == 0, own_part, other_part)
-    up_pre = jnp.where(core == 0, other_part, own_part)
+    sent = lax.dot_general(theirs, mine, DIMS, preferred_element_type=jnp.float32)
+    other = swapped(sent, "core", 1)
+    own = lax.dot_general(normed, mine, DIMS, preferred_element_type=jnp.float32)
+    gate_pre = jnp.where(core == 0, own, other)
+    up_pre = jnp.where(core == 0, other, own)
     return (jax.nn.silu(gate_pre) * up_pre).astype(jnp.bfloat16)[None]
 
 

time: 180 us -> 172 us (0.956)
  waiting for transfers between devices: 78.4 us -> 41.4 us
  other arithmetic: 13.4 us -> 30.3 us
  starting transfers between devices: 25.7 us -> 32.4 us
  Pallas kernels: 0 us -> 6.56 us
  matrix products: 32.6 us -> 30.7 us
    all_gather x1, waiting for transfers between devices: 28.3 us -> 8.31 us  [gathered_weights(): return lax.all_gather(block, ('x', 'z'), axis=0, tiled=True)]
    ppermute x11 -> x13, waiting for transfers between devices: 43.4 us -> 27.3 us  [swapped(): lax.ppermute(value, axis, [(i, i ^ mask) for i in range(lax.axis_size(axi...]
    pallas_call x0 -> x1, Pallas kernels: none -> 6.56 us  [mixed_and_normed(): pl.pallas_call(mix_kernel, grid=(width // cut,), in_specs=[column, pl.Blo...]
    ppermute x11 -> x13, starting transfers between devices: 22.9 us -> 29.1 us  [swapped(): lax.ppermute(value, axis, [(i, i ^ mask) for i in range(lax.axis_size(axi...]
    unnamed x0 -> x5, other arithmetic: none -> 5.74 us
    dot_general x8 -> x2, matrix products: 17.8 us -> 12.6 us  [the longest x1 6.31 us: per_device(): lax.dot_general(theirs, mine, DIMS, preferred_element_type=jnp.float32)]
    concatenate x0 -> x6, other arithmetic: none -> 3.73 us  [the longest x3 2.01 us: joined(): return jnp.concatenate(pair, axis=1)]
    select_n x2 -> x3, other arithmetic: 1.35 us -> 4.52 us  [joined(): jnp.where(place == 0, own, theirs)]
  transfers between devices with their start and end apart: 15 -> 17, of which waited for: 11 -> 11; matrix products, arithmetic and copies ran while one was open for 27% -> 37% of each run, Pallas kernels for 0% -> 4%
where the time goes in v3:
time: 172 us; the launch traced here: 171 us
  waiting for transfers between devices  41.4 us (24%)
  starting transfers between devices  32.4 us (19%)
  matrix products  30.7 us (18%)
  other arithmetic  30.3 us (18%)
  local copies, waits for them, and re-layouts  15.5 us (9%)
  between operations  14.6 us (8%)
  Pallas kernels  6.56 us (4%)
    ppermute x13, starting transfers between devices, swapped(): lax.ppermute(value, axis, [(i, i ^ mask) for i in range(lax.axis_size(axi...  29.1 us
    ppermute x13, waiting for transfers between devices, swapped(): lax.ppermute(value, axis, [(i, i ^ mask) for i in range(lax.axis_size(axi...  27.3 us
    dot_general x1, matrix products, local_mix(): chosen = jnp.einsum('lht,lts->hts', mix_low, level_picks, precision=HIGH)  9.14 us
    all_gather x1, waiting for transfers between devices, gathered_weights(): return lax.all_gather(block, ('x', 'z'), axis=0, tiled=True)  8.31 us
    dot_general x1, matrix products, local_mix(): jnp.einsum('hts,shp->thp', weights, x_blk, preferred_element_type=jnp.flo...  6.62 us
    pallas_call x1, Pallas kernels, mixed_and_normed(): pl.pallas_call(mix_kernel, grid=(width // cut,), in_specs=[column, pl.Blo...  6.56 us
    dot_general x1, matrix products, per_device(): lax.dot_general(theirs, mine, DIMS, preferred_element_type=jnp.float32)  6.31 us
    dot_general x1, matrix products, per_device(): lax.dot_general(normed, mine, DIMS, preferred_element_type=jnp.float32)  6.31 us
  transfers between devices with their start and end apart: 17, of which 11 were waited for; matrix products, arithmetic and copies ran while one was open for 37% of the time, Pallas kernels for 4%

profile of v3, /device:TPU:1, one launch (start us, length us, event | category | flops | bytes accessed | tf_op | source)
XLA Modules:
  0.0 171.5 jit_solution(4713954148247533170)
XLA Ops:
  7.4 3.3 %collective-permute-start.10 = (bf16[11,2048]{1,0:T(8,128)(2,1)S(1)}, bf16[11,2048]{1,0:T(8,128)(2,1)S(1)}, u32[]{:S(2)}, u32[]{:S(2)}) collective-permute-start(bf16[11,2048]{1,0:T(8,128)(2,1)S(1)} %select_bitcast_fusion.4), channel_id=1, source_target_pairs={{0,4},{4,0},{1,5},{5,1},{2,6},{6,2},{3,7},{7,3},{8,12},{12,8},{9,1... | collective-permute-start | bytes 135176 | tf_op jit(solution)/shard_map/ppermute | solution.py:20
  12.6 2.2 %collective-permute-start.12 = (bf16[2,11,2048]{2,1,0:T(8,128)(2,1)S(1)}, bf16[2,11,2048]{2,1,0:T(8,128)(2,1)S(1)}, u32[]{:S(2)}, u32[]{:S(2)}) collective-permute-start(bf16[2,11,2048]{2,1,0:T(8,128)(2,1)S(1)} %pad_maximum_fusion.6), channel_id=1, source_target_pairs={{0,2},{1,3},{2,0},{3,1},{4,6},{5,7},{6,4},{7,5},{8,10},{9,11},{10,... | collective-permute-start | bytes 270344 | tf_op jit(solution)/shard_map/ppermute | solution.py:25
  15.9 3.2 %collective-permute-done.11 = bf16[2,11,2048]{2,1,0:T(8,128)(2,1)S(1)} collective-permute-done((bf16[2,11,2048]{2,1,0:T(8,128)(2,1)S(1)}, bf16[2,11,2048]{2,1,0:T(8,128)(2,1)S(1)}, u32[]{:S(2)}, u32[]{:S(2)}) %collective-permute-start.11) | collective-permute-done | bytes 90144 | tf_op jit(solution)/shard_map/ppermute | solution.py:25
  19.0 1.9 %collective-permute-done.12 = bf16[2,11,2048]{2,1,0:T(8,128)(2,1)S(1)} collective-permute-done((bf16[2,11,2048]{2,1,0:T(8,128)(2,1)S(1)}, bf16[2,11,2048]{2,1,0:T(8,128)(2,1)S(1)}, u32[]{:S(2)}, u32[]{:S(2)}) %collective-permute-start.12) | collective-permute-done | bytes 90144 | tf_op jit(solution)/shard_map/ppermute | solution.py:25
  38.1 7.6 %collective-permute-done.1 = bf16[1032,128]{1,0:T(8,128)(2,1)S(1)} collective-permute-done((bf16[1032,128]{1,0:T(8,128)(2,1)S(1)}, bf16[1032,128]{1,0:T(8,128)(2,1)S(1)}, u32[]{:S(2)}, u32[]{:S(2)}) %collective-permute-start.1) | collective-permute-done | bytes 264224 | tf_op jit(solution)/shard_map/ppermute | solution.py:20
  47.1 2.4 %collective-permute-start.2 = (bf16[520,128]{1,0:T(8,128)(2,1)S(1)}, bf16[520,128]{1,0:T(8,128)(2,1)S(1)}, u32[]{:S(2)}, u32[]{:S(2)}) collective-permute-start(bf16[520,128]{1,0:T(8,128)(2,1)S(1)} %fusion.31), channel_id=1, source_target_pairs={{0,16},{8,24},{16,0},{24,8},{32,48},{40,56},{48,32},{56,40},{1,17}... | collective-permute-start | bytes 399368 | tf_op jit(solution)/shard_map/ppermute | solution.py:20
  50.3 2.5 %copy.58 = f32[1,9,32,256]{2,1,3,0:T(8,128)} copy(f32[1,9,32,256]{3,2,1,0:T(8,128)S(1)} %slice-done) | data formatting | bytes 589824 | tf_op jit(solution)/shard_map/slice | solution.py:214
  58.2 9.4 %collective-permute-start.3 = (bf16[520,128]{1,0:T(8,128)(2,1)S(1)}, bf16[520,128]{1,0:T(8,128)(2,1)S(1)}, u32[]{:S(2)}, u32[]{:S(2)}) collective-permute-start(bf16[520,128]{1,0:T(8,128)(2,1)S(1)} %fusion.32), channel_id=1, source_target_pairs={{0,32},{8,40},{16,48},{24,56},{32,0},{40,8},{48,16},{56,24},{1,33}... | collective-permute-start | bytes 399368 | tf_op jit(solution)/shard_map/ppermute | solution.py:20
  67.6 9.1 %fusion.1 = bf16[32,256,256]{2,0,1:T(8,128)(2,1)} fusion(f32[256,256]{1,0:T(8,128)S(1)} %copy-done.15, f32[32,256]{1,0:T(8,128)S(1)} %copy_bitcast_fusion, f32[32,256]{0,1:T(8,128)S(1)} %copy.59, pred[256,256]{1,0:T(8,128)(4,1)S(1)} %iota_compare_fusion.7, f32[1,9,32,256]{2,1,3,0:T(8,128)} %copy.58, s32[256,256]{1,0:T(8,128)} %add_select_fusion, ...), kind=kOutput, calls=%fused_computation.2 | convolution fusion | flops 237641728 | bytes 5144580 | tf_op jit(solution)/shard_map/lht,lts->hts/dot_general | solution.py:42
  78.2 2.1 %collective-permute-start.6 = (bf16[520,128]{1,0:T(8,128)(2,1)}, bf16[520,128]{1,0:T(8,128)(2,1)}, u32[]{:S(2)}, u32[]{:S(2)}) collective-permute-start(bf16[520,128]{1,0:T(8,128)(2,1)} %fusion.33), channel_id=1, source_target_pairs={{0,64},{64,0},{128,192},{192,128},{1,65},{65,1},{129,193},{193,129... | collective-permute-start | bytes 399368 | tf_op jit(solution)/shard_map/ppermute | solution.py:20
  80.3 6.6 %fusion.2 = f32[32,256,64]{1,2,0:T(8,128)} fusion(bf16[256,32,64]{0,2,1:T(8,128)(2,1)S(1)} %bitcast.218, bf16[32,256,256]{2,0,1:T(8,128)(2,1)} %fusion.1), kind=kOutput, calls=%fused_computation.5 | convolution fusion | flops 268435456 | bytes 7340032 | tf_op jit(solution)/shard_map/hts,shp->thp/dot_general | solution.py:47
  87.0 1.9 %copy.61.local = f32[256,2048]{1,0:T(8,128)S(1)} copy(f32[256,2048]{0,1:T(8,128)} %bitcast.216) | data formatting | bytes 4194304 | tf_op jit(solution)/shard_map/reshape | solution.py:220
  93.5 2.6 %collective-permute-start.7 = (bf16[520,128]{1,0:T(8,128)(2,1)S(1)}, bf16[520,128]{1,0:T(8,128)(2,1)S(1)}, u32[]{:S(2)}, u32[]{:S(2)}) collective-permute-start(bf16[520,128]{1,0:T(8,128)(2,1)S(1)} %fusion.34), channel_id=1, source_target_pairs={{0,128},{64,192},{128,0},{192,64},{1,129},{65,193},{129,1},{193,65... | collective-permute-start | bytes 399368 | tf_op jit(solution)/shard_map/ppermute | solution.py:20
  97.6 5.1 %collective-permute-done.7 = bf16[520,128]{1,0:T(8,128)(2,1)S(1)} collective-permute-done((bf16[520,128]{1,0:T(8,128)(2,1)S(1)}, bf16[520,128]{1,0:T(8,128)(2,1)S(1)}, u32[]{:S(2)}, u32[]{:S(2)}) %collective-permute-start.7) | collective-permute-done | bytes 133152 | tf_op jit(solution)/shard_map/ppermute | solution.py:20
  107.2 8.3 %collective-permute-done.8 = bf16[2,8,64,128]{3,2,1,0:T(8,128)(2,1)S(1)} collective-permute-done((bf16[2,8,64,128]{3,2,1,0:T(8,128)(2,1)S(1)}, bf16[2,8,64,128]{3,2,1,0:T(8,128)(2,1)S(1)}, u32[]{:S(2)}, u32[]{:S(2)}) %collective-permute-start.8) | collective-permute-done | bytes 262176 | tf_op jit(solution)/shard_map/ppermute | solution.py:20
  115.4 1.7 %broadcast_select_fusion.5 = (bf16[2,8,64,128]{3,2,1,0:T(8,128)(2,1)}, bf16[2,8,64,128]{3,2,1,0:T(8,128)(2,1)S(1)}, bf16[2,8,64,128]{3,2,1,0:T(8,128)(2,1)S(1)}, bf16[2,8,64,128]{3,2,1,0:T(8,128)(2,1)S(1)}) fusion(bf16[2,8,64,128]{3,2,1,0:T(8,128)(2,1)S(1)} %collective-permute-done.8, pred[]{:T(512)S(6)} %eq.98, bf16[1,8,64,128]{3,2,1,0:T(8,128)(2,1)S(1)} %bitcast.236, ...), kind=kLoop, calls=%fused_computation.66 | loop fusion | flops 786432 | bytes 2097153 | tf_op jit(solution)/shard_map/jit(_where)/select_n | solution.py:204
  117.9 1.8 %pad_maximum_fusion.2 = bf16[2,16,64,128]{3,2,1,0:T(8,128)(2,1)} fusion(bf16[2,8,64,128]{3,2,1,0:T(8,128)(2,1)S(1)} %get-tuple-element.38, bf16[2,8,64,128]{3,2,1,0:T(8,128)(2,1)} %get-tuple-element.37), kind=kLoop, calls=%fused_computation.32 | loop fusion | flops 262144 | bytes 1048576 | tf_op jit(solution)/shard_map/concatenate | solution.py:205
  119.7 3.8 %collective-permute-start.9 = (bf16[2,16,64,128]{3,2,1,0:T(8,128)(2,1)}, bf16[2,16,64,128]{3,2,1,0:T(8,128)(2,1)}, u32[]{:S(2)}, u32[]{:S(2)}) collective-permute-start(bf16[2,16,64,128]{3,2,1,0:T(8,128)(2,1)} %pad_maximum_fusion.2), channel_id=1, source_target_pairs={{0,4},{4,0},{1,5},{5,1},{2,6},{6,2},{3,7},{7,3},{8,12},{12,8},{9,1... | collective-permute-start | bytes 1572872 | tf_op jit(solution)/shard_map/ppermute | solution.py:20
  130.1 6.6 %shard_map.91 = bf16[256,2048]{1,0:T(8,128)(2,1)S(1)} custom-call(f32[256,2048]{1,0:T(8,128)S(1)} %copy.61.local, bf16[2048,128]{1,0:T(8,128)(2,1)S(1)} %slice.207.first, bf16[3,2048,128]{2,1,0:T(8,128)(2,1)S(1)} %bitcast.211, bf16[2,2048,128]{2,1,0:T(8,128)(2,1)S(1)} %bitcast.212, bf16[256,128]{1,0:T(8,128)(2,1)S(1)} %bitcast.214, ...), custom_call_target="tpu_custom_call" | custom-call | flops 939524096 | bytes 8388608 | tf_op jit(solution)/shard_map/pallas_call | solution.py:125
  138.2 2.3 %collective-permute-done.14 = bf16[256,2048]{1,0:T(8,128)(2,1)S(1)} collective-permute-done((bf16[256,2048]{1,0:T(8,128)(2,1)S(1)}, bf16[256,2048]{1,0:T(8,128)(2,1)S(1)}, u32[]{:S(2)}, u32[]{:S(2)}) %collective-permute-start.14) | collective-permute-done | bytes 1048608 | tf_op jit(solution)/shard_map/ppermute | solution.py:20
  140.5 8.3 %all-gather.2.cloned.1.call-done = bf16[2816,2048]{1,0:T(8,128)(2,1)} async-done(((bf16[88,2048]{1,0:T(8,128)(2,1)}), bf16[2816,2048]{1,0:T(8,128)(2,1)}) %all-gather.2.cloned.1.call-update) | async-done | bytes 11534352 | tf_op jit(solution)/shard_map/all_gather | solution.py:82
  148.8 6.3 %fusion.60 = f32[256,2816]{1,0:T(8,128)S(1)} fusion(bf16[256,2048]{1,0:T(8,128)(2,1)S(1)} %collective-permute-done.14, bf16[2816,2048]{1,0:T(8,128)(2,1)} %all-gather.2.cloned.1.call-done), kind=kOutput, calls=%fused_computation.175 | convolution fusion | flops 2952790016 | bytes 15466496 | tf_op jit(solution)/shard_map/dot_general | solution.py:230
  156.4 6.3 %fusion.59 = f32[256,2816]{1,0:T(8,128)S(1)} fusion(bf16[256,2048]{1,0:T(8,128)(2,1)S(1)} %copy-done.2, bf16[2816,2048]{1,0:T(8,128)(2,1)} %all-gather.2.cloned.1.call-done), kind=kOutput, calls=%fused_computation.174 | convolution fusion | flops 2952790016 | bytes 15466496 | tf_op jit(solution)/shard_map/dot_general | solution.py:232
  162.7 1.9 %fusion.11 = bf16[1,256,2816]{2,1,0:T(8,128)(2,1)} fusion(f32[256,2816]{1,0:T(8,128)S(1)} %collective-permute-done.15, f32[256,2816]{1,0:T(8,128)S(1)} %fusion.59, pred[]{:T(512)S(6)} %eq.94), kind=kLoop, calls=%fused_computation.18 | loop fusion | flops 5767168 | bytes 7208961 | tf_op jit(solution)/shard_map/broadcast_in_dim | solution.py:235
  (170 shorter events, 49.7 us)
Async XLA Ops:
  6.5 142.3 %all-gather.2.cloned.1.call-start = ((), (), s32[]{:S(2)}) async-start(), calls=%async_computation | async-start | bytes 11894784 | tf_op jit(solution)/shard_map/all_gather | solution.py:82
  6.5 16.3 %copy-start.17 = (f32[1,32,256]{2,1,0:T(8,128)S(1)}, f32[1,32,256]{2,1,0:T(8,128)}, u32[]{:S(2)}) copy-start(f32[1,32,256]{2,1,0:T(8,128)} %param.13) | copy-start | bytes 98308
  7.4 4.2 %collective-permute-start.10 = (bf16[11,2048]{1,0:T(8,128)(2,1)S(1)}, bf16[11,2048]{1,0:T(8,128)(2,1)S(1)}, u32[]{:S(2)}, u32[]{:S(2)}) collective-permute-start(bf16[11,2048]{1,0:T(8,128)(2,1)S(1)} %select_bitcast_fusion.4), channel_id=1, source_target_pairs={{0,4},{4,0},{1,5},{5,1},{2,6},{6,2},{3,7},{7,3},{8,12},{12,8},{9,1... | collective-permute-start | bytes 135176 | tf_op jit(solution)/shard_map/ppermute | solution.py:20
  12.5 6.5 %collective-permute-start.11 = (bf16[2,11,2048]{2,1,0:T(8,128)(2,1)S(1)}, bf16[2,11,2048]{2,1,0:T(8,128)(2,1)S(1)}, u32[]{:S(2)}, u32[]{:S(2)}) collective-permute-start(bf16[2,11,2048]{2,1,0:T(8,128)(2,1)S(1)} %pad_maximum_fusion.6), channel_id=1, source_target_pairs={{0,1},{1,2},{2,3},{3,0},{4,5},{5,6},{6,7},{7,4},{8,9},{9,10},{10,1... | collective-permute-start | bytes 270344 | tf_op jit(solution)/shard_map/ppermute | solution.py:25
  12.6 8.3 %collective-permute-start.12 = (bf16[2,11,2048]{2,1,0:T(8,128)(2,1)S(1)}, bf16[2,11,2048]{2,1,0:T(8,128)(2,1)S(1)}, u32[]{:S(2)}, u32[]{:S(2)}) collective-permute-start(bf16[2,11,2048]{2,1,0:T(8,128)(2,1)S(1)} %pad_maximum_fusion.6), channel_id=1, source_target_pairs={{0,2},{1,3},{2,0},{3,1},{4,6},{5,7},{6,4},{7,5},{8,10},{9,11},{10,... | collective-permute-start | bytes 270344 | tf_op jit(solution)/shard_map/ppermute | solution.py:25
  14.8 6.8 %collective-permute-start.13 = (bf16[2,11,2048]{2,1,0:T(8,128)(2,1)S(1)}, bf16[2,11,2048]{2,1,0:T(8,128)(2,1)S(1)}, u32[]{:S(2)}, u32[]{:S(2)}) collective-permute-start(bf16[2,11,2048]{2,1,0:T(8,128)(2,1)S(1)} %pad_maximum_fusion.6), channel_id=1, source_target_pairs={{0,3},{1,0},{2,1},{3,2},{4,7},{5,4},{6,5},{7,6},{8,11},{9,8},{10,9... | collective-permute-start | bytes 270344 | tf_op jit(solution)/shard_map/ppermute | solution.py:25
  27.1 4.1 %collective-permute-start = (f32[2056,128]{1,0:T(8,128)}, f32[2056,128]{1,0:T(8,128)}, u32[]{:S(2)}, u32[]{:S(2)}) collective-permute-start(f32[2056,128]{1,0:T(8,128)} %select_maximum_fusion), channel_id=1, source_target_pairs={{0,4},{4,0},{1,5},{5,1},{2,6},{6,2},{3,7},{7,3},{8,12},{12,8},{9,1... | collective-permute-start | bytes 3158024 | tf_op jit(solution)/shard_map/ppermute | solution.py:20
  35.8 9.9 %collective-permute-start.1 = (bf16[1032,128]{1,0:T(8,128)(2,1)S(1)}, bf16[1032,128]{1,0:T(8,128)(2,1)S(1)}, u32[]{:S(2)}, u32[]{:S(2)}) collective-permute-start(bf16[1032,128]{1,0:T(8,128)(2,1)S(1)} %fusion.20), channel_id=1, source_target_pairs={{0,8},{8,0},{16,24},{24,16},{32,40},{40,32},{48,56},{56,48},{1,9},... | collective-permute-start | bytes 792584 | tf_op jit(solution)/shard_map/ppermute | solution.py:20
  45.9 77.5 %copy-start.5 = (bf16[1024,128]{1,0:T(8,128)(2,1)}, bf16[1024,128]{1,0:T(8,128)(2,1)S(1)}, u32[]{:S(2)}) copy-start(bf16[1024,128]{1,0:T(8,128)(2,1)S(1)} %slice.168) | copy-start | bytes 786436
  47.1 9.8 %collective-permute-start.2 = (bf16[520,128]{1,0:T(8,128)(2,1)S(1)}, bf16[520,128]{1,0:T(8,128)(2,1)S(1)}, u32[]{:S(2)}, u32[]{:S(2)}) collective-permute-start(bf16[520,128]{1,0:T(8,128)(2,1)S(1)} %fusion.31), channel_id=1, source_target_pairs={{0,16},{8,24},{16,0},{24,8},{32,48},{40,56},{48,32},{56,40},{1,17}... | collective-permute-start | bytes 399368 | tf_op jit(solution)/shard_map/ppermute | solution.py:20
  50.2 17.4 %copy-start.15 = (f32[256,256]{1,0:T(8,128)S(1)}, f32[256,256]{1,0:T(8,128)}, u32[]{:S(2)}) copy-start(f32[256,256]{1,0:T(8,128)} %fusion.37) | copy-start | bytes 786436
  56.9 19.9 %copy-start.18 = (f32[1,32]{1,0:T(1,128)}, f32[1,32]{1,0:T(1,128)S(1)}, u32[]{:S(2)}) copy-start(f32[1,32]{1,0:T(1,128)S(1)} %get-tuple-element.19) | copy-start | bytes 388
  56.9 19.9 %copy-start.22 = (f32[32]{0:T(128)}, f32[32]{0:T(128)S(1)}, u32[]{:S(2)}) copy-start(f32[32]{0:T(128)S(1)} %get-tuple-element.18) | copy-start | bytes 388
  58.2 18.5 %collective-permute-start.3 = (bf16[520,128]{1,0:T(8,128)(2,1)S(1)}, bf16[520,128]{1,0:T(8,128)(2,1)S(1)}, u32[]{:S(2)}, u32[]{:S(2)}) collective-permute-start(bf16[520,128]{1,0:T(8,128)(2,1)S(1)} %fusion.32), channel_id=1, source_target_pairs={{0,32},{8,40},{16,48},{24,56},{32,0},{40,8},{48,16},{56,24},{1,33}... | collective-permute-start | bytes 399368 | tf_op jit(solution)/shard_map/ppermute | solution.py:20
  78.2 11.4 %collective-permute-start.6 = (bf16[520,128]{1,0:T(8,128)(2,1)}, bf16[520,128]{1,0:T(8,128)(2,1)}, u32[]{:S(2)}, u32[]{:S(2)}) collective-permute-start(bf16[520,128]{1,0:T(8,128)(2,1)} %fusion.33), channel_id=1, source_target_pairs={{0,64},{64,0},{128,192},{192,128},{1,65},{65,1},{129,193},{193,129... | collective-permute-start | bytes 399368 | tf_op jit(solution)/shard_map/ppermute | solution.py:20
  89.6 17.5 %collective-permute-start.4 = (bf16[2,8,64,128]{3,2,1,0:T(8,128)(2,1)}, bf16[2,8,64,128]{3,2,1,0:T(8,128)(2,1)}, u32[]{:S(2)}, u32[]{:S(2)}) collective-permute-start(bf16[2,8,64,128]{3,2,1,0:T(8,128)(2,1)} %pad_maximum_fusion.4), channel_id=1, source_target_pairs={{0,8},{8,0},{16,24},{24,16},{32,40},{40,32},{48,56},{56,48},{1,9},... | collective-permute-start | bytes 786440 | tf_op jit(solution)/shard_map/ppermute | solution.py:20
  93.5 9.2 %collective-permute-start.7 = (bf16[520,128]{1,0:T(8,128)(2,1)S(1)}, bf16[520,128]{1,0:T(8,128)(2,1)S(1)}, u32[]{:S(2)}, u32[]{:S(2)}) collective-permute-start(bf16[520,128]{1,0:T(8,128)(2,1)S(1)} %fusion.34), channel_id=1, source_target_pairs={{0,128},{64,192},{128,0},{192,64},{1,129},{65,193},{129,1},{193,65... | collective-permute-start | bytes 399368 | tf_op jit(solution)/shard_map/ppermute | solution.py:20
  97.6 26.8 %copy-start.13 = (f32[1,15,32,256]{3,2,1,0:T(8,128)S(1)}, f32[1,15,32,256]{3,2,1,0:T(8,128)}, u32[]{:S(2)}) copy-start(f32[1,15,32,256]{3,2,1,0:T(8,128)} %param.14) | copy-start | bytes 1474564
  102.7 12.7 %collective-permute-start.8 = (bf16[2,8,64,128]{3,2,1,0:T(8,128)(2,1)S(1)}, bf16[2,8,64,128]{3,2,1,0:T(8,128)(2,1)S(1)}, u32[]{:S(2)}, u32[]{:S(2)}) collective-permute-start(bf16[2,8,64,128]{3,2,1,0:T(8,128)(2,1)S(1)} %pad_maximum_fusion.5), channel_id=1, source_target_pairs={{0,8},{8,0},{16,24},{24,16},{32,40},{40,32},{48,56},{56,48},{1,9},... | collective-permute-start | bytes 786440 | tf_op jit(solution)/shard_map/ppermute | solution.py:20
  119.7 7.4 %collective-permute-start.9 = (bf16[2,16,64,128]{3,2,1,0:T(8,128)(2,1)}, bf16[2,16,64,128]{3,2,1,0:T(8,128)(2,1)}, u32[]{:S(2)}, u32[]{:S(2)}) collective-permute-start(bf16[2,16,64,128]{3,2,1,0:T(8,128)(2,1)} %pad_maximum_fusion.2), channel_id=1, source_target_pairs={{0,4},{4,0},{1,5},{5,1},{2,6},{6,2},{3,7},{7,3},{8,12},{12,8},{9,1... | collective-permute-start | bytes 1572872 | tf_op jit(solution)/shard_map/ppermute | solution.py:20
  124.4 4.1 %collective-permute-start.5 = (bf16[3,16,64,128]{3,2,1,0:T(8,128)(2,1)}, bf16[3,16,64,128]{3,2,1,0:T(8,128)(2,1)}, u32[]{:S(2)}, u32[]{:S(2)}) collective-permute-start(bf16[3,16,64,128]{3,2,1,0:T(8,128)(2,1)} %maximum_maximum_fusion), channel_id=1, source_target_pairs={{0,4},{4,0},{1,5},{5,1},{2,6},{6,2},{3,7},{7,3},{8,12},{12,8},{9,1... | collective-permute-start | bytes 2359304 | tf_op jit(solution)/shard_map/ppermute | solution.py:20
  137.7 2.8 %collective-permute-start.14 = (bf16[256,2048]{1,0:T(8,128)(2,1)S(1)}, bf16[256,2048]{1,0:T(8,128)(2,1)S(1)}, u32[]{:S(2)}, u32[]{:S(2)}) collective-permute-start(bf16[256,2048]{1,0:T(8,128)(2,1)S(1)} %shard_map.91), channel_id=1, source_target_pairs={{0,4},{4,0},{1,5},{5,1},{2,6},{6,2},{3,7},{7,3},{8,12},{12,8},{9,1... | collective-permute-start | bytes 3145736 | tf_op jit(solution)/shard_map/ppermute | solution.py:20
  138.2 18.2 %copy-start.2 = (bf16[256,2048]{1,0:T(8,128)(2,1)S(1)}, bf16[256,2048]{1,0:T(8,128)(2,1)}, u32[]{:S(2)}) copy-start(bf16[256,2048]{1,0:T(8,128)(2,1)} %copy-done.1) | copy-start | bytes 3145732
  155.1 7.6 %collective-permute-start.15 = (f32[256,2816]{1,0:T(8,128)S(1)}, f32[256,2816]{1,0:T(8,128)S(1)}, u32[]{:S(2)}, u32[]{:S(2)}) collective-permute-start(f32[256,2816]{1,0:T(8,128)S(1)} %fusion.60), channel_id=1, source_target_pairs={{0,4},{4,0},{1,5},{5,1},{2,6},{6,2},{3,7},{7,3},{8,12},{12,8},{9,1... | collective-permute-start | bytes 8650760 | tf_op jit(solution)/shard_map/ppermute | solution.py:20
  (20 other events, 113.2 us)
Sparse Core Ops, SparseCore 0:
  22.9 125.8 all-gather.1

commit v4 on v3

--- a/solution.py
+++ b/solution.py
@@ -16,8 +16,9 @@
 DIMS = (((1,), (1,)), ((), ()))
 
 
-def swapped(value, axis, mask):
-    return lax.ppermute(value, axis, [(i, i ^ mask) for i in range(lax.axis_size(axis))])
+def swapped(value, axis, mask, senders=None):
+    places = range(lax.axis_size(axis)) if senders is None else senders
+    return lax.ppermute(value, axis, [(i, i ^ mask) for i in places])
 
 
 def shifted(value, axis, step):
@@ -180,7 +181,8 @@
     quarter = half // 2
     odd = lax.axis_index("z") & 1
     for bit, (axis, mask) in enumerate(STEPS, 1):
-        received = swapped(packed(summary, total, jnp.bfloat16), axis, mask)
+        senders = range(mask) if bit == len(STEPS) else None
+        received = swapped(packed(summary, total, jnp.bfloat16), axis, mask, senders)
         levels.append(received[:-8])
         their_state, their_decay = unpacked(received, heads)
         is_upper = here >> bit & 1 == 1
@@ -199,15 +201,16 @@
             prefix = jnp.where(is_upper, prefix + their_decay, prefix)
             total = total + their_decay
 
-    def joined(own, axis, place):
-        theirs = swapped(own, axis, 1)
+    def joined(own, axis, place, senders=None):
+        theirs = swapped(own, axis, 1, senders)
         pair = (jnp.where(place == 0, own, theirs), jnp.where(place == 0, theirs, own))
         return jnp.concatenate(pair, axis=1)
 
     def split(rows):
         return rows.reshape(1, -1, head_dim, rows.shape[1])
 
-    near = joined(jnp.concatenate([split(levels[1]), split(levels[2])]), "z", odd)
+    steps = range(2, lax.axis_size("z"))
+    near = joined(jnp.concatenate([split(levels[1]), split(levels[2])]), "z", odd, steps)
     near = joined(jnp.concatenate([split(levels[0]), near]), "core", core)
     far = joined(jnp.concatenate([split(levels[3]), split(levels[4])]), "z", odd)
     far = joined(far, "core", core)

time: 172 us -> 171 us (level)
  waiting for transfers between devices: 41.4 us -> 38.7 us
    all_gather x1, waiting for transfers between devices: 8.31 us -> 4.95 us  [gathered_weights(): return lax.all_gather(block, ('x', 'z'), axis=0, tiled=True)]
where the time goes in v4:
time: 171 us; the launch traced here: 170 us
  waiting for transfers between devices  38.7 us (23%)
  starting transfers between devices  33.6 us (20%)
  matrix products  30.7 us (18%)
  other arithmetic  30.3 us (18%)
  local copies, waits for them, and re-layouts  15.6 us (9%)
  between operations  14.6 us (9%)
  Pallas kernels  6.57 us (4%)
    ppermute x13, starting transfers between devices, swapped(): return lax.ppermute(value, axis, [(i, i ^ mask) for i in places])  30.3 us
    ppermute x13, waiting for transfers between devices, swapped(): return lax.ppermute(value, axis, [(i, i ^ mask) for i in places])  28 us
    dot_general x1, matrix products, local_mix(): chosen = jnp.einsum('lht,lts->hts', mix_low, level_picks, precision=HIGH)  9.14 us
    dot_general x1, matrix products, local_mix(): jnp.einsum('hts,shp->thp', weights, x_blk, preferred_element_type=jnp.flo...  6.62 us
    pallas_call x1, Pallas kernels, mixed_and_normed(): pl.pallas_call(mix_kernel, grid=(width // cut,), in_specs=[column, pl.Blo...  6.57 us
    dot_general x1, matrix products, per_device(): lax.dot_general(theirs, mine, DIMS, preferred_element_type=jnp.float32)  6.31 us
    dot_general x1, matrix products, per_device(): lax.dot_general(normed, mine, DIMS, preferred_element_type=jnp.float32)  6.31 us
    ppermute x3, waiting for transfers between devices, shifted(): lax.ppermute(value, axis, [(i, (i + step) % count) for i in range(count)])  5.75 us
  transfers between devices with their start and end apart: 17, of which 11 were waited for; matrix products, arithmetic and copies ran while one was open for 37% of the time, Pallas kernels for 4%

profile of v4, /device:TPU:1, one launch (start us, length us, event | category | flops | bytes accessed | tf_op | source)
XLA Modules:
  0.0 170.0 jit_solution(902848701063727684)
XLA Ops:
  7.4 3.3 %collective-permute-start.10 = (bf16[11,2048]{1,0:T(8,128)(2,1)S(1)}, bf16[11,2048]{1,0:T(8,128)(2,1)S(1)}, u32[]{:S(2)}, u32[]{:S(2)}) collective-permute-start(bf16[11,2048]{1,0:T(8,128)(2,1)S(1)} %select_bitcast_fusion.4), channel_id=1, source_target_pairs={{0,4},{4,0},{1,5},{5,1},{2,6},{6,2},{3,7},{7,3},{8,12},{12,8},{9,1... | collective-permute-start | bytes 135176 | tf_op jit(solution)/shard_map/ppermute | solution.py:21
  12.6 2.2 %collective-permute-start.12 = (bf16[2,11,2048]{2,1,0:T(8,128)(2,1)S(1)}, bf16[2,11,2048]{2,1,0:T(8,128)(2,1)S(1)}, u32[]{:S(2)}, u32[]{:S(2)}) collective-permute-start(bf16[2,11,2048]{2,1,0:T(8,128)(2,1)S(1)} %pad_maximum_fusion.6), channel_id=1, source_target_pairs={{0,2},{1,3},{2,0},{3,1},{4,6},{5,7},{6,4},{7,5},{8,10},{9,11},{10,... | collective-permute-start | bytes 270344 | tf_op jit(solution)/shard_map/ppermute | solution.py:26
  15.9 3.2 %collective-permute-done.11 = bf16[2,11,2048]{2,1,0:T(8,128)(2,1)S(1)} collective-permute-done((bf16[2,11,2048]{2,1,0:T(8,128)(2,1)S(1)}, bf16[2,11,2048]{2,1,0:T(8,128)(2,1)S(1)}, u32[]{:S(2)}, u32[]{:S(2)}) %collective-permute-start.11) | collective-permute-done | bytes 90144 | tf_op jit(solution)/shard_map/ppermute | solution.py:26
  19.0 1.9 %collective-permute-done.12 = bf16[2,11,2048]{2,1,0:T(8,128)(2,1)S(1)} collective-permute-done((bf16[2,11,2048]{2,1,0:T(8,128)(2,1)S(1)}, bf16[2,11,2048]{2,1,0:T(8,128)(2,1)S(1)}, u32[]{:S(2)}, u32[]{:S(2)}) %collective-permute-start.12) | collective-permute-done | bytes 90144 | tf_op jit(solution)/shard_map/ppermute | solution.py:26
  38.1 7.6 %collective-permute-done.1 = bf16[1032,128]{1,0:T(8,128)(2,1)S(1)} collective-permute-done((bf16[1032,128]{1,0:T(8,128)(2,1)S(1)}, bf16[1032,128]{1,0:T(8,128)(2,1)S(1)}, u32[]{:S(2)}, u32[]{:S(2)}) %collective-permute-start.1) | collective-permute-done | bytes 264224 | tf_op jit(solution)/shard_map/ppermute | solution.py:21
  47.1 2.4 %collective-permute-start.2 = (bf16[520,128]{1,0:T(8,128)(2,1)S(1)}, bf16[520,128]{1,0:T(8,128)(2,1)S(1)}, u32[]{:S(2)}, u32[]{:S(2)}) collective-permute-start(bf16[520,128]{1,0:T(8,128)(2,1)S(1)} %fusion.31), channel_id=1, source_target_pairs={{0,16},{8,24},{16,0},{24,8},{32,48},{40,56},{48,32},{56,40},{1,17}... | collective-permute-start | bytes 399368 | tf_op jit(solution)/shard_map/ppermute | solution.py:21
  50.3 2.5 %copy.58 = f32[1,9,32,256]{2,1,3,0:T(8,128)} copy(f32[1,9,32,256]{3,2,1,0:T(8,128)S(1)} %slice-done) | data formatting | bytes 589824 | tf_op jit(solution)/shard_map/slice | solution.py:217
  58.2 9.4 %collective-permute-start.3 = (bf16[520,128]{1,0:T(8,128)(2,1)S(1)}, bf16[520,128]{1,0:T(8,128)(2,1)S(1)}, u32[]{:S(2)}, u32[]{:S(2)}) collective-permute-start(bf16[520,128]{1,0:T(8,128)(2,1)S(1)} %fusion.32), channel_id=1, source_target_pairs={{0,32},{8,40},{16,48},{24,56},{32,0},{40,8},{48,16},{56,24},{1,33}... | collective-permute-start | bytes 399368 | tf_op jit(solution)/shard_map/ppermute | solution.py:21
  67.6 9.1 %fusion.1 = bf16[32,256,256]{2,0,1:T(8,128)(2,1)} fusion(f32[256,256]{1,0:T(8,128)S(1)} %copy-done.15, f32[32,256]{1,0:T(8,128)S(1)} %copy_bitcast_fusion, f32[32,256]{0,1:T(8,128)S(1)} %copy.59, pred[256,256]{1,0:T(8,128)(4,1)S(1)} %iota_compare_fusion.7, f32[1,9,32,256]{2,1,3,0:T(8,128)} %copy.58, s32[256,256]{1,0:T(8,128)} %add_select_fusion, ...), kind=kOutput, calls=%fused_computation.2 | convolution fusion | flops 237641728 | bytes 5144580 | tf_op jit(solution)/shard_map/lht,lts->hts/dot_general | solution.py:43
  78.2 2.1 %collective-permute-start.6 = (bf16[520,128]{1,0:T(8,128)(2,1)}, bf16[520,128]{1,0:T(8,128)(2,1)}, u32[]{:S(2)}, u32[]{:S(2)}) collective-permute-start(bf16[520,128]{1,0:T(8,128)(2,1)} %fusion.33), channel_id=1, source_target_pairs={{0,64},{64,0},{128,192},{192,128},{1,65},{65,1},{129,193},{193,129... | collective-permute-start | bytes 399368 | tf_op jit(solution)/shard_map/ppermute | solution.py:21
  80.3 6.6 %fusion.2 = f32[32,256,64]{1,2,0:T(8,128)} fusion(bf16[256,32,64]{0,2,1:T(8,128)(2,1)S(1)} %bitcast.218, bf16[32,256,256]{2,0,1:T(8,128)(2,1)} %fusion.1), kind=kOutput, calls=%fused_computation.5 | convolution fusion | flops 268435456 | bytes 7340032 | tf_op jit(solution)/shard_map/hts,shp->thp/dot_general | solution.py:48
  87.0 1.9 %copy.61.local = f32[256,2048]{1,0:T(8,128)S(1)} copy(f32[256,2048]{0,1:T(8,128)} %bitcast.216) | data formatting | bytes 4194304 | tf_op jit(solution)/shard_map/reshape | solution.py:223
  94.9 4.5 %collective-permute-start.7 = (bf16[520,128]{1,0:T(8,128)(2,1)S(1)}, bf16[520,128]{1,0:T(8,128)(2,1)S(1)}, u32[]{:S(2)}, u32[]{:S(2)}) collective-permute-start(bf16[520,128]{1,0:T(8,128)(2,1)S(1)} %fusion.34), channel_id=1, source_target_pairs={{0,128},{64,192},{1,129},{65,193},{2,130},{66,194},{3,131},{67,195... | collective-permute-start | bytes 399368 | tf_op jit(solution)/shard_map/ppermute | solution.py:21
  100.8 4.0 %collective-permute-done.7 = bf16[520,128]{1,0:T(8,128)(2,1)S(1)} collective-permute-done((bf16[520,128]{1,0:T(8,128)(2,1)S(1)}, bf16[520,128]{1,0:T(8,128)(2,1)S(1)}, u32[]{:S(2)}, u32[]{:S(2)}) %collective-permute-start.7) | collective-permute-done | bytes 133152 | tf_op jit(solution)/shard_map/ppermute | solution.py:21
  107.8 10.1 %collective-permute-done.8 = bf16[2,8,64,128]{3,2,1,0:T(8,128)(2,1)S(1)} collective-permute-done((bf16[2,8,64,128]{3,2,1,0:T(8,128)(2,1)S(1)}, bf16[2,8,64,128]{3,2,1,0:T(8,128)(2,1)S(1)}, u32[]{:S(2)}, u32[]{:S(2)}) %collective-permute-start.8) | collective-permute-done | bytes 262176 | tf_op jit(solution)/shard_map/ppermute | solution.py:21
  117.9 1.7 %broadcast_select_fusion.5 = (bf16[2,8,64,128]{3,2,1,0:T(8,128)(2,1)}, bf16[2,8,64,128]{3,2,1,0:T(8,128)(2,1)S(1)}, bf16[2,8,64,128]{3,2,1,0:T(8,128)(2,1)S(1)}, bf16[2,8,64,128]{3,2,1,0:T(8,128)(2,1)S(1)}) fusion(bf16[2,8,64,128]{3,2,1,0:T(8,128)(2,1)S(1)} %collective-permute-done.8, pred[]{:T(512)S(6)} %eq.98, bf16[1,8,64,128]{3,2,1,0:T(8,128)(2,1)S(1)} %bitcast.236, ...), kind=kLoop, calls=%fused_computation.66 | loop fusion | flops 786432 | bytes 2097153 | tf_op jit(solution)/shard_map/jit(_where)/select_n | solution.py:206
  120.3 1.8 %pad_maximum_fusion.2 = bf16[2,16,64,128]{3,2,1,0:T(8,128)(2,1)} fusion(bf16[2,8,64,128]{3,2,1,0:T(8,128)(2,1)S(1)} %get-tuple-element.38, bf16[2,8,64,128]{3,2,1,0:T(8,128)(2,1)} %get-tuple-element.37), kind=kLoop, calls=%fused_computation.32 | loop fusion | flops 262144 | bytes 1048576 | tf_op jit(solution)/shard_map/concatenate | solution.py:207
  122.1 3.3 %collective-permute-start.9 = (bf16[2,16,64,128]{3,2,1,0:T(8,128)(2,1)}, bf16[2,16,64,128]{3,2,1,0:T(8,128)(2,1)}, u32[]{:S(2)}, u32[]{:S(2)}) collective-permute-start(bf16[2,16,64,128]{3,2,1,0:T(8,128)(2,1)} %pad_maximum_fusion.2), channel_id=1, source_target_pairs={{0,4},{4,0},{1,5},{5,1},{2,6},{6,2},{3,7},{7,3},{8,12},{12,8},{9,1... | collective-permute-start | bytes 1572872 | tf_op jit(solution)/shard_map/ppermute | solution.py:21
  132.2 6.6 %shard_map.91 = bf16[256,2048]{1,0:T(8,128)(2,1)S(1)} custom-call(f32[256,2048]{1,0:T(8,128)S(1)} %copy.61.local, bf16[2048,128]{1,0:T(8,128)(2,1)S(1)} %slice.207.first, bf16[3,2048,128]{2,1,0:T(8,128)(2,1)S(1)} %bitcast.211, bf16[2,2048,128]{2,1,0:T(8,128)(2,1)S(1)} %bitcast.212, bf16[256,128]{1,0:T(8,128)(2,1)S(1)} %bitcast.214, ...), custom_call_target="tpu_custom_call" | custom-call | flops 939524096 | bytes 8388608 | tf_op jit(solution)/shard_map/pallas_call | solution.py:126
  140.2 2.3 %collective-permute-done.14 = bf16[256,2048]{1,0:T(8,128)(2,1)S(1)} collective-permute-done((bf16[256,2048]{1,0:T(8,128)(2,1)S(1)}, bf16[256,2048]{1,0:T(8,128)(2,1)S(1)}, u32[]{:S(2)}, u32[]{:S(2)}) %collective-permute-start.14) | collective-permute-done | bytes 1048608 | tf_op jit(solution)/shard_map/ppermute | solution.py:21
  142.5 4.9 %all-gather.2.cloned.1.call-done = bf16[2816,2048]{1,0:T(8,128)(2,1)} async-done(((bf16[88,2048]{1,0:T(8,128)(2,1)}), bf16[2816,2048]{1,0:T(8,128)(2,1)}) %all-gather.2.cloned.1.call-update) | async-done | bytes 11534352 | tf_op jit(solution)/shard_map/all_gather | solution.py:83
  147.5 6.3 %fusion.60 = f32[256,2816]{1,0:T(8,128)S(1)} fusion(bf16[256,2048]{1,0:T(8,128)(2,1)S(1)} %collective-permute-done.14, bf16[2816,2048]{1,0:T(8,128)(2,1)} %all-gather.2.cloned.1.call-done), kind=kOutput, calls=%fused_computation.175 | convolution fusion | flops 2952790016 | bytes 15466496 | tf_op jit(solution)/shard_map/dot_general | solution.py:233
  154.9 6.3 %fusion.59 = f32[256,2816]{1,0:T(8,128)S(1)} fusion(bf16[256,2048]{1,0:T(8,128)(2,1)S(1)} %copy-done.2, bf16[2816,2048]{1,0:T(8,128)(2,1)} %all-gather.2.cloned.1.call-done), kind=kOutput, calls=%fused_computation.174 | convolution fusion | flops 2952790016 | bytes 15466496 | tf_op jit(solution)/shard_map/dot_general | solution.py:235
  161.2 1.9 %fusion.11 = bf16[1,256,2816]{2,1,0:T(8,128)(2,1)} fusion(f32[256,2816]{1,0:T(8,128)S(1)} %collective-permute-done.15, f32[256,2816]{1,0:T(8,128)S(1)} %fusion.59, pred[]{:T(512)S(6)} %eq.94), kind=kLoop, calls=%fused_computation.18 | loop fusion | flops 5767168 | bytes 7208961 | tf_op jit(solution)/shard_map/broadcast_in_dim | solution.py:238
  (170 shorter events, 49.4 us)
Async XLA Ops:
  6.5 140.9 %all-gather.2.cloned.1.call-start = ((), (), s32[]{:S(2)}) async-start(), calls=%async_computation | async-start | bytes 11894784 | tf_op jit(solution)/shard_map/all_gather | solution.py:83
  6.5 16.3 %copy-start.17 = (f32[1,32,256]{2,1,0:T(8,128)S(1)}, f32[1,32,256]{2,1,0:T(8,128)}, u32[]{:S(2)}) copy-start(f32[1,32,256]{2,1,0:T(8,128)} %param.13) | copy-start | bytes 98308
  7.4 16.2 %copy-start.14 = (bf16[1,256,2048]{2,1,0:T(8,128)(2,1)S(1)}, bf16[1,256,2048]{2,1,0:T(8,128)(2,1)}, u32[]{:S(2)}) copy-start(bf16[1,256,2048]{2,1,0:T(8,128)(2,1)} %param.9) | copy-start | bytes 3145732
  7.4 4.2 %collective-permute-start.10 = (bf16[11,2048]{1,0:T(8,128)(2,1)S(1)}, bf16[11,2048]{1,0:T(8,128)(2,1)S(1)}, u32[]{:S(2)}, u32[]{:S(2)}) collective-permute-start(bf16[11,2048]{1,0:T(8,128)(2,1)S(1)} %select_bitcast_fusion.4), channel_id=1, source_target_pairs={{0,4},{4,0},{1,5},{5,1},{2,6},{6,2},{3,7},{7,3},{8,12},{12,8},{9,1... | collective-permute-start | bytes 135176 | tf_op jit(solution)/shard_map/ppermute | solution.py:21
  12.5 6.5 %collective-permute-start.11 = (bf16[2,11,2048]{2,1,0:T(8,128)(2,1)S(1)}, bf16[2,11,2048]{2,1,0:T(8,128)(2,1)S(1)}, u32[]{:S(2)}, u32[]{:S(2)}) collective-permute-start(bf16[2,11,2048]{2,1,0:T(8,128)(2,1)S(1)} %pad_maximum_fusion.6), channel_id=1, source_target_pairs={{0,1},{1,2},{2,3},{3,0},{4,5},{5,6},{6,7},{7,4},{8,9},{9,10},{10,1... | collective-permute-start | bytes 270344 | tf_op jit(solution)/shard_map/ppermute | solution.py:26
  12.6 8.3 %collective-permute-start.12 = (bf16[2,11,2048]{2,1,0:T(8,128)(2,1)S(1)}, bf16[2,11,2048]{2,1,0:T(8,128)(2,1)S(1)}, u32[]{:S(2)}, u32[]{:S(2)}) collective-permute-start(bf16[2,11,2048]{2,1,0:T(8,128)(2,1)S(1)} %pad_maximum_fusion.6), channel_id=1, source_target_pairs={{0,2},{1,3},{2,0},{3,1},{4,6},{5,7},{6,4},{7,5},{8,10},{9,11},{10,... | collective-permute-start | bytes 270344 | tf_op jit(solution)/shard_map/ppermute | solution.py:26
  14.8 6.8 %collective-permute-start.13 = (bf16[2,11,2048]{2,1,0:T(8,128)(2,1)S(1)}, bf16[2,11,2048]{2,1,0:T(8,128)(2,1)S(1)}, u32[]{:S(2)}, u32[]{:S(2)}) collective-permute-start(bf16[2,11,2048]{2,1,0:T(8,128)(2,1)S(1)} %pad_maximum_fusion.6), channel_id=1, source_target_pairs={{0,3},{1,0},{2,1},{3,2},{4,7},{5,4},{6,5},{7,6},{8,11},{9,8},{10,9... | collective-permute-start | bytes 270344 | tf_op jit(solution)/shard_map/ppermute | solution.py:26
  27.1 4.1 %collective-permute-start = (f32[2056,128]{1,0:T(8,128)}, f32[2056,128]{1,0:T(8,128)}, u32[]{:S(2)}, u32[]{:S(2)}) collective-permute-start(f32[2056,128]{1,0:T(8,128)} %select_maximum_fusion), channel_id=1, source_target_pairs={{0,4},{4,0},{1,5},{5,1},{2,6},{6,2},{3,7},{7,3},{8,12},{12,8},{9,1... | collective-permute-start | bytes 3158024 | tf_op jit(solution)/shard_map/ppermute | solution.py:21
  35.8 9.9 %collective-permute-start.1 = (bf16[1032,128]{1,0:T(8,128)(2,1)S(1)}, bf16[1032,128]{1,0:T(8,128)(2,1)S(1)}, u32[]{:S(2)}, u32[]{:S(2)}) collective-permute-start(bf16[1032,128]{1,0:T(8,128)(2,1)S(1)} %fusion.20), channel_id=1, source_target_pairs={{0,8},{8,0},{16,24},{24,16},{32,40},{40,32},{48,56},{56,48},{1,9},... | collective-permute-start | bytes 792584 | tf_op jit(solution)/shard_map/ppermute | solution.py:21
  45.9 79.6 %copy-start.5 = (bf16[1024,128]{1,0:T(8,128)(2,1)}, bf16[1024,128]{1,0:T(8,128)(2,1)S(1)}, u32[]{:S(2)}) copy-start(bf16[1024,128]{1,0:T(8,128)(2,1)S(1)} %slice.168) | copy-start | bytes 786436
  47.1 9.8 %collective-permute-start.2 = (bf16[520,128]{1,0:T(8,128)(2,1)S(1)}, bf16[520,128]{1,0:T(8,128)(2,1)S(1)}, u32[]{:S(2)}, u32[]{:S(2)}) collective-permute-start(bf16[520,128]{1,0:T(8,128)(2,1)S(1)} %fusion.31), channel_id=1, source_target_pairs={{0,16},{8,24},{16,0},{24,8},{32,48},{40,56},{48,32},{56,40},{1,17}... | collective-permute-start | bytes 399368 | tf_op jit(solution)/shard_map/ppermute | solution.py:21
  50.2 17.4 %copy-start.15 = (f32[256,256]{1,0:T(8,128)S(1)}, f32[256,256]{1,0:T(8,128)}, u32[]{:S(2)}) copy-start(f32[256,256]{1,0:T(8,128)} %fusion.37) | copy-start | bytes 786436
  56.9 19.9 %copy-start.18 = (f32[1,32]{1,0:T(1,128)}, f32[1,32]{1,0:T(1,128)S(1)}, u32[]{:S(2)}) copy-start(f32[1,32]{1,0:T(1,128)S(1)} %get-tuple-element.19) | copy-start | bytes 388
  56.9 19.9 %copy-start.22 = (f32[32]{0:T(128)}, f32[32]{0:T(128)S(1)}, u32[]{:S(2)}) copy-start(f32[32]{0:T(128)S(1)} %get-tuple-element.18) | copy-start | bytes 388
  58.2 18.5 %collective-permute-start.3 = (bf16[520,128]{1,0:T(8,128)(2,1)S(1)}, bf16[520,128]{1,0:T(8,128)(2,1)S(1)}, u32[]{:S(2)}, u32[]{:S(2)}) collective-permute-start(bf16[520,128]{1,0:T(8,128)(2,1)S(1)} %fusion.32), channel_id=1, source_target_pairs={{0,32},{8,40},{16,48},{24,56},{32,0},{40,8},{48,16},{56,24},{1,33}... | collective-permute-start | bytes 399368 | tf_op jit(solution)/shard_map/ppermute | solution.py:21
  78.2 12.7 %collective-permute-start.6 = (bf16[520,128]{1,0:T(8,128)(2,1)}, bf16[520,128]{1,0:T(8,128)(2,1)}, u32[]{:S(2)}, u32[]{:S(2)}) collective-permute-start(bf16[520,128]{1,0:T(8,128)(2,1)} %fusion.33), channel_id=1, source_target_pairs={{0,64},{64,0},{128,192},{192,128},{1,65},{65,1},{129,193},{193,129... | collective-permute-start | bytes 399368 | tf_op jit(solution)/shard_map/ppermute | solution.py:21
  89.6 18.2 %collective-permute-start.4 = (bf16[2,8,64,128]{3,2,1,0:T(8,128)(2,1)}, bf16[2,8,64,128]{3,2,1,0:T(8,128)(2,1)}, u32[]{:S(2)}, u32[]{:S(2)}) collective-permute-start(bf16[2,8,64,128]{3,2,1,0:T(8,128)(2,1)} %pad_maximum_fusion.4), channel_id=1, source_target_pairs={{16,24},{24,16},{32,40},{40,32},{48,56},{56,48},{17,25},{25,17},{3... | collective-permute-start | bytes 786440 | tf_op jit(solution)/shard_map/ppermute | solution.py:21
  94.9 9.9 %collective-permute-start.7 = (bf16[520,128]{1,0:T(8,128)(2,1)S(1)}, bf16[520,128]{1,0:T(8,128)(2,1)S(1)}, u32[]{:S(2)}, u32[]{:S(2)}) collective-permute-start(bf16[520,128]{1,0:T(8,128)(2,1)S(1)} %fusion.34), channel_id=1, source_target_pairs={{0,128},{64,192},{1,129},{65,193},{2,130},{66,194},{3,131},{67,195... | collective-permute-start | bytes 399368 | tf_op jit(solution)/shard_map/ppermute | solution.py:21
  100.8 25.6 %copy-start.13 = (f32[1,15,32,256]{3,2,1,0:T(8,128)S(1)}, f32[1,15,32,256]{3,2,1,0:T(8,128)}, u32[]{:S(2)}) copy-start(f32[1,15,32,256]{3,2,1,0:T(8,128)} %param.14) | copy-start | bytes 1474564
  104.8 13.1 %collective-permute-start.8 = (bf16[2,8,64,128]{3,2,1,0:T(8,128)(2,1)S(1)}, bf16[2,8,64,128]{3,2,1,0:T(8,128)(2,1)S(1)}, u32[]{:S(2)}, u32[]{:S(2)}) collective-permute-start(bf16[2,8,64,128]{3,2,1,0:T(8,128)(2,1)S(1)} %pad_maximum_fusion.5), channel_id=1, source_target_pairs={{0,8},{8,0},{16,24},{24,16},{32,40},{40,32},{48,56},{56,48},{1,9},... | collective-permute-start | bytes 786440 | tf_op jit(solution)/shard_map/ppermute | solution.py:21
  122.1 6.9 %collective-permute-start.9 = (bf16[2,16,64,128]{3,2,1,0:T(8,128)(2,1)}, bf16[2,16,64,128]{3,2,1,0:T(8,128)(2,1)}, u32[]{:S(2)}, u32[]{:S(2)}) collective-permute-start(bf16[2,16,64,128]{3,2,1,0:T(8,128)(2,1)} %pad_maximum_fusion.2), channel_id=1, source_target_pairs={{0,4},{4,0},{1,5},{5,1},{2,6},{6,2},{3,7},{7,3},{8,12},{12,8},{9,1... | collective-permute-start | bytes 1572872 | tf_op jit(solution)/shard_map/ppermute | solution.py:21
  126.4 4.1 %collective-permute-start.5 = (bf16[3,16,64,128]{3,2,1,0:T(8,128)(2,1)}, bf16[3,16,64,128]{3,2,1,0:T(8,128)(2,1)}, u32[]{:S(2)}, u32[]{:S(2)}) collective-permute-start(bf16[3,16,64,128]{3,2,1,0:T(8,128)(2,1)} %maximum_maximum_fusion), channel_id=1, source_target_pairs={{0,4},{4,0},{1,5},{5,1},{2,6},{6,2},{3,7},{7,3},{8,12},{12,8},{9,1... | collective-permute-start | bytes 2359304 | tf_op jit(solution)/shard_map/ppermute | solution.py:21
  139.7 2.8 %collective-permute-start.14 = (bf16[256,2048]{1,0:T(8,128)(2,1)S(1)}, bf16[256,2048]{1,0:T(8,128)(2,1)S(1)}, u32[]{:S(2)}, u32[]{:S(2)}) collective-permute-start(bf16[256,2048]{1,0:T(8,128)(2,1)S(1)} %shard_map.91), channel_id=1, source_target_pairs={{0,4},{4,0},{1,5},{5,1},{2,6},{6,2},{3,7},{7,3},{8,12},{12,8},{9,1... | collective-permute-start | bytes 3145736 | tf_op jit(solution)/shard_map/ppermute | solution.py:21
  153.8 7.4 %collective-permute-start.15 = (f32[256,2816]{1,0:T(8,128)S(1)}, f32[256,2816]{1,0:T(8,128)S(1)}, u32[]{:S(2)}, u32[]{:S(2)}) collective-permute-start(f32[256,2816]{1,0:T(8,128)S(1)} %fusion.60), channel_id=1, source_target_pairs={{0,4},{4,0},{1,5},{5,1},{2,6},{6,2},{3,7},{7,3},{8,12},{12,8},{9,1... | collective-permute-start | bytes 8650760 | tf_op jit(solution)/shard_map/ppermute | solution.py:21
  (20 other events, 114.8 us)
Sparse Core Ops, SparseCore 0:
  22.9 124.5 all-gather.1

commit v5 on v4

--- a/solution.py
+++ b/solution.py
@@ -181,7 +181,7 @@
     quarter = half // 2
     odd = lax.axis_index("z") & 1
     for bit, (axis, mask) in enumerate(STEPS, 1):
-        senders = range(mask) if bit == len(STEPS) else None
+        senders = range(mask) if bit == len(STEPS) else range(3) if bit == len(STEPS) - 1 else None
         received = swapped(packed(summary, total, jnp.bfloat16), axis, mask, senders)
         levels.append(received[:-8])
         their_state, their_decay = unpacked(received, heads)
@@ -212,7 +212,9 @@
     steps = range(2, lax.axis_size("z"))
     near = joined(jnp.concatenate([split(levels[1]), split(levels[2])]), "z", odd, steps)
     near = joined(jnp.concatenate([split(levels[0]), near]), "core", core)
-    far = joined(jnp.concatenate([split(levels[3]), split(levels[4])]), "z", odd)
+    depth = lax.axis_size("z")
+    steps = range(depth, lax.axis_size("x") * depth)
+    far = joined(jnp.concatenate([split(levels[3]), split(levels[4])]), ("x", "z"), odd, steps)
     far = joined(far, "core", core)
     local = local_mix(x_blk, b_blk, c_blk, running, mix[:inner] + levels[0][:1, :1] * 0)
     scales = []

time: 171 us -> 171 us (level); the launches traced: 170 us -> 168 us
  waiting for transfers between devices: 38.7 us -> 34.3 us
  starting transfers between devices: 33.6 us -> 36.1 us
    ppermute x13, waiting for transfers between devices: 28 us -> 17.9 us  [swapped(): return lax.ppermute(value, axis, [(i, i ^ mask) for i in places])]
    all_gather x1, waiting for transfers between devices: 4.95 us -> 10.7 us  [gathered_weights(): return lax.all_gather(block, ('x', 'z'), axis=0, tiled=True)]
    ppermute x13, starting transfers between devices: 30.3 us -> 32.7 us  [swapped(): return lax.ppermute(value, axis, [(i, i ^ mask) for i in places])]
  transfers between devices with their start and end apart: 17 -> 17, of which waited for: 11 -> 10; matrix products, arithmetic and copies ran while one was open for 37% -> 37% of each run, Pallas kernels for 4% -> 4%
where the time goes in v5:
time: 171 us; the launch traced here: 168 us
  starting transfers between devices  36.1 us (21%)
  waiting for transfers between devices  34.3 us (20%)
  other arithmetic  30.4 us (18%)
  matrix products  30.2 us (18%)
  local copies, waits for them, and re-layouts  15.5 us (9%)
  between operations  14.6 us (9%)
  Pallas kernels  6.56 us (4%)
    ppermute x13, starting transfers between devices, swapped(): return lax.ppermute(value, axis, [(i, i ^ mask) for i in places])  32.7 us
    ppermute x13, waiting for transfers between devices, swapped(): return lax.ppermute(value, axis, [(i, i ^ mask) for i in places])  17.9 us
    all_gather x1, waiting for transfers between devices, gathered_weights(): return lax.all_gather(block, ('x', 'z'), axis=0, tiled=True)  10.7 us
    dot_general x1, matrix products, local_mix(): chosen = jnp.einsum('lht,lts->hts', mix_low, level_picks, precision=HIGH)  9.14 us
    pallas_call x1, Pallas kernels, mixed_and_normed(): pl.pallas_call(mix_kernel, grid=(width // cut,), in_specs=[column, pl.Blo...  6.56 us
    dot_general x1, matrix products, per_device(): lax.dot_general(normed, mine, DIMS, preferred_element_type=jnp.float32)  6.31 us
    dot_general x1, matrix products, per_device(): lax.dot_general(theirs, mine, DIMS, preferred_element_type=jnp.float32)  6.31 us
    dot_general x1, matrix products, local_mix(): jnp.einsum('hts,shp->thp', weights, x_blk, preferred_element_type=jnp.flo...  6.15 us
  transfers between devices with their start and end apart: 17, of which 10 were waited for; matrix products, arithmetic and copies ran while one was open for 37% of the time, Pallas kernels for 4%

profile of v5, /device:TPU:1, one launch (start us, length us, event | category | flops | bytes accessed | tf_op | source)
XLA Modules:
  0.0 167.7 jit_solution(11913078649526430189)
XLA Ops:
  7.4 3.3 %collective-permute-start.10 = (bf16[11,2048]{1,0:T(8,128)(2,1)S(1)}, bf16[11,2048]{1,0:T(8,128)(2,1)S(1)}, u32[]{:S(2)}, u32[]{:S(2)}) collective-permute-start(bf16[11,2048]{1,0:T(8,128)(2,1)S(1)} %select_bitcast_fusion.4), channel_id=1, source_target_pairs={{0,4},{4,0},{1,5},{5,1},{2,6},{6,2},{3,7},{7,3},{8,12},{12,8},{9,1... | collective-permute-start | bytes 135176 | tf_op jit(solution)/shard_map/ppermute | solution.py:21
  12.6 2.2 %collective-permute-start.12 = (bf16[2,11,2048]{2,1,0:T(8,128)(2,1)S(1)}, bf16[2,11,2048]{2,1,0:T(8,128)(2,1)S(1)}, u32[]{:S(2)}, u32[]{:S(2)}) collective-permute-start(bf16[2,11,2048]{2,1,0:T(8,128)(2,1)S(1)} %pad_maximum_fusion.6), channel_id=1, source_target_pairs={{0,2},{1,3},{2,0},{3,1},{4,6},{5,7},{6,4},{7,5},{8,10},{9,11},{10,... | collective-permute-start | bytes 270344 | tf_op jit(solution)/shard_map/ppermute | solution.py:26
  15.9 3.2 %collective-permute-done.11 = bf16[2,11,2048]{2,1,0:T(8,128)(2,1)S(1)} collective-permute-done((bf16[2,11,2048]{2,1,0:T(8,128)(2,1)S(1)}, bf16[2,11,2048]{2,1,0:T(8,128)(2,1)S(1)}, u32[]{:S(2)}, u32[]{:S(2)}) %collective-permute-start.11) | collective-permute-done | bytes 90144 | tf_op jit(solution)/shard_map/ppermute | solution.py:26
  19.0 1.9 %collective-permute-done.12 = bf16[2,11,2048]{2,1,0:T(8,128)(2,1)S(1)} collective-permute-done((bf16[2,11,2048]{2,1,0:T(8,128)(2,1)S(1)}, bf16[2,11,2048]{2,1,0:T(8,128)(2,1)S(1)}, u32[]{:S(2)}, u32[]{:S(2)}) %collective-permute-start.12) | collective-permute-done | bytes 90144 | tf_op jit(solution)/shard_map/ppermute | solution.py:26
  38.1 7.6 %collective-permute-done.1 = bf16[1032,128]{1,0:T(8,128)(2,1)S(1)} collective-permute-done((bf16[1032,128]{1,0:T(8,128)(2,1)S(1)}, bf16[1032,128]{1,0:T(8,128)(2,1)S(1)}, u32[]{:S(2)}, u32[]{:S(2)}) %collective-permute-start.1) | collective-permute-done | bytes 264224 | tf_op jit(solution)/shard_map/ppermute | solution.py:21
  47.1 2.4 %collective-permute-start.2 = (bf16[520,128]{1,0:T(8,128)(2,1)S(1)}, bf16[520,128]{1,0:T(8,128)(2,1)S(1)}, u32[]{:S(2)}, u32[]{:S(2)}) collective-permute-start(bf16[520,128]{1,0:T(8,128)(2,1)S(1)} %fusion.31), channel_id=1, source_target_pairs={{0,16},{8,24},{16,0},{24,8},{32,48},{40,56},{48,32},{56,40},{1,17}... | collective-permute-start | bytes 399368 | tf_op jit(solution)/shard_map/ppermute | solution.py:21
  50.3 2.5 %copy.58 = f32[1,9,32,256]{2,1,3,0:T(8,128)} copy(f32[1,9,32,256]{3,2,1,0:T(8,128)S(1)} %slice-done) | data formatting | bytes 589824 | tf_op jit(solution)/shard_map/slice | solution.py:219
  55.3 1.6 collective-permute-done.2
  58.2 9.4 %collective-permute-start.3 = (bf16[520,128]{1,0:T(8,128)(2,1)S(1)}, bf16[520,128]{1,0:T(8,128)(2,1)S(1)}, u32[]{:S(2)}, u32[]{:S(2)}) collective-permute-start(bf16[520,128]{1,0:T(8,128)(2,1)S(1)} %fusion.32), channel_id=1, source_target_pairs={{0,32},{8,40},{16,48},{24,56},{32,0},{40,8},{48,16},{56,24},{1,33}... | collective-permute-start | bytes 399368 | tf_op jit(solution)/shard_map/ppermute | solution.py:21
  67.6 9.1 %fusion.1 = bf16[32,256,256]{2,0,1:T(8,128)(2,1)} fusion(f32[256,256]{1,0:T(8,128)S(1)} %copy-done.15, f32[32,256]{1,0:T(8,128)S(1)} %copy_bitcast_fusion, f32[32,256]{0,1:T(8,128)S(1)} %copy.59, pred[256,256]{1,0:T(8,128)(4,1)S(1)} %iota_compare_fusion.7, f32[1,9,32,256]{2,1,3,0:T(8,128)} %copy.58, s32[256,256]{1,0:T(8,128)} %add_select_fusion, ...), kind=kOutput, calls=%fused_computation.2 | convolution fusion | flops 237641728 | bytes 5144580 | tf_op jit(solution)/shard_map/lht,lts->hts/dot_general | solution.py:43
  78.2 4.0 %collective-permute-start.6 = (bf16[520,128]{1,0:T(8,128)(2,1)}, bf16[520,128]{1,0:T(8,128)(2,1)}, u32[]{:S(2)}, u32[]{:S(2)}) collective-permute-start(bf16[520,128]{1,0:T(8,128)(2,1)} %fusion.33), channel_id=1, source_target_pairs={{0,64},{64,0},{128,192},{1,65},{65,1},{129,193},{2,66},{66,2},{130... | collective-permute-start | bytes 399368 | tf_op jit(solution)/shard_map/ppermute | solution.py:21
  82.2 6.1 %fusion.2 = f32[32,256,64]{1,2,0:T(8,128)} fusion(bf16[256,32,64]{0,2,1:T(8,128)(2,1)S(1)} %bitcast.218, bf16[32,256,256]{2,0,1:T(8,128)(2,1)} %fusion.1), kind=kOutput, calls=%fused_computation.5 | convolution fusion | flops 268435456 | bytes 7340032 | tf_op jit(solution)/shard_map/hts,shp->thp/dot_general | solution.py:48
  88.4 1.9 %copy.61.local = f32[256,2048]{1,0:T(8,128)S(1)} copy(f32[256,2048]{0,1:T(8,128)} %bitcast.216) | data formatting | bytes 4194304 | tf_op jit(solution)/shard_map/reshape | solution.py:225
  96.3 5.1 %collective-permute-start.7 = (bf16[520,128]{1,0:T(8,128)(2,1)S(1)}, bf16[520,128]{1,0:T(8,128)(2,1)S(1)}, u32[]{:S(2)}, u32[]{:S(2)}) collective-permute-start(bf16[520,128]{1,0:T(8,128)(2,1)S(1)} %fusion.34), channel_id=1, source_target_pairs={{0,128},{64,192},{1,129},{65,193},{2,130},{66,194},{3,131},{67,195... | collective-permute-start | bytes 399368 | tf_op jit(solution)/shard_map/ppermute | solution.py:21
  102.9 3.9 %collective-permute-done.7 = bf16[520,128]{1,0:T(8,128)(2,1)S(1)} collective-permute-done((bf16[520,128]{1,0:T(8,128)(2,1)S(1)}, bf16[520,128]{1,0:T(8,128)(2,1)S(1)}, u32[]{:S(2)}, u32[]{:S(2)}) %collective-permute-start.7) | collective-permute-done | bytes 133152 | tf_op jit(solution)/shard_map/ppermute | solution.py:21
  110.5 1.7 %broadcast_select_fusion.5 = (bf16[2,8,64,128]{3,2,1,0:T(8,128)(2,1)}, bf16[2,8,64,128]{3,2,1,0:T(8,128)(2,1)S(1)}, bf16[2,8,64,128]{3,2,1,0:T(8,128)(2,1)S(1)}, bf16[2,8,64,128]{3,2,1,0:T(8,128)(2,1)S(1)}) fusion(bf16[2,8,64,128]{3,2,1,0:T(8,128)(2,1)S(1)} %collective-permute-done.8, pred[]{:T(512)S(6)} %eq.98, bf16[1,8,64,128]{3,2,1,0:T(8,128)(2,1)S(1)} %bitcast.236, ...), kind=kLoop, calls=%fused_computation.66 | loop fusion | flops 786432 | bytes 2097153 | tf_op jit(solution)/shard_map/jit(_where)/select_n | solution.py:206
  112.9 1.8 %pad_maximum_fusion.2 = bf16[2,16,64,128]{3,2,1,0:T(8,128)(2,1)} fusion(bf16[2,8,64,128]{3,2,1,0:T(8,128)(2,1)S(1)} %get-tuple-element.38, bf16[2,8,64,128]{3,2,1,0:T(8,128)(2,1)} %get-tuple-element.37), kind=kLoop, calls=%fused_computation.32 | loop fusion | flops 262144 | bytes 1048576 | tf_op jit(solution)/shard_map/concatenate | solution.py:207
  114.7 2.7 %collective-permute-start.9 = (bf16[2,16,64,128]{3,2,1,0:T(8,128)(2,1)}, bf16[2,16,64,128]{3,2,1,0:T(8,128)(2,1)}, u32[]{:S(2)}, u32[]{:S(2)}) collective-permute-start(bf16[2,16,64,128]{3,2,1,0:T(8,128)(2,1)} %pad_maximum_fusion.2), channel_id=1, source_target_pairs={{0,4},{4,0},{1,5},{5,1},{2,6},{6,2},{3,7},{7,3},{8,12},{12,8},{9,1... | collective-permute-start | bytes 1572872 | tf_op jit(solution)/shard_map/ppermute | solution.py:21
  124.2 6.6 %shard_map.91 = bf16[256,2048]{1,0:T(8,128)(2,1)S(1)} custom-call(f32[256,2048]{1,0:T(8,128)S(1)} %copy.61.local, bf16[2048,128]{1,0:T(8,128)(2,1)S(1)} %slice.207.first, bf16[3,2048,128]{2,1,0:T(8,128)(2,1)S(1)} %bitcast.211, bf16[2,2048,128]{2,1,0:T(8,128)(2,1)S(1)} %bitcast.212, bf16[256,128]{1,0:T(8,128)(2,1)S(1)} %bitcast.214, ...), custom_call_target="tpu_custom_call" | custom-call | flops 939524096 | bytes 8388608 | tf_op jit(solution)/shard_map/pallas_call | solution.py:126
  132.3 2.3 %collective-permute-done.14 = bf16[256,2048]{1,0:T(8,128)(2,1)S(1)} collective-permute-done((bf16[256,2048]{1,0:T(8,128)(2,1)S(1)}, bf16[256,2048]{1,0:T(8,128)(2,1)S(1)}, u32[]{:S(2)}, u32[]{:S(2)}) %collective-permute-start.14) | collective-permute-done | bytes 1048608 | tf_op jit(solution)/shard_map/ppermute | solution.py:21
  134.6 10.7 %all-gather.2.cloned.1.call-done = bf16[2816,2048]{1,0:T(8,128)(2,1)} async-done(((bf16[88,2048]{1,0:T(8,128)(2,1)}), bf16[2816,2048]{1,0:T(8,128)(2,1)}) %all-gather.2.cloned.1.call-update) | async-done | bytes 11534352 | tf_op jit(solution)/shard_map/all_gather | solution.py:83
  145.3 6.3 %fusion.60 = f32[256,2816]{1,0:T(8,128)S(1)} fusion(bf16[256,2048]{1,0:T(8,128)(2,1)S(1)} %collective-permute-done.14, bf16[2816,2048]{1,0:T(8,128)(2,1)} %all-gather.2.cloned.1.call-done), kind=kOutput, calls=%fused_computation.175 | convolution fusion | flops 2952790016 | bytes 15466496 | tf_op jit(solution)/shard_map/dot_general | solution.py:235
  152.6 6.3 %fusion.59 = f32[256,2816]{1,0:T(8,128)S(1)} fusion(bf16[256,2048]{1,0:T(8,128)(2,1)S(1)} %copy-done.2, bf16[2816,2048]{1,0:T(8,128)(2,1)} %all-gather.2.cloned.1.call-done), kind=kOutput, calls=%fused_computation.174 | convolution fusion | flops 2952790016 | bytes 15466496 | tf_op jit(solution)/shard_map/dot_general | solution.py:237
  159.0 1.9 %fusion.11 = bf16[1,256,2816]{2,1,0:T(8,128)(2,1)} fusion(f32[256,2816]{1,0:T(8,128)S(1)} %collective-permute-done.15, f32[256,2816]{1,0:T(8,128)S(1)} %fusion.59, pred[]{:T(512)S(6)} %eq.94), kind=kLoop, calls=%fused_computation.18 | loop fusion | flops 5767168 | bytes 7208961 | tf_op jit(solution)/shard_map/broadcast_in_dim | solution.py:240
  (170 shorter events, 48.5 us)
Async XLA Ops:
  6.5 138.7 %all-gather.2.cloned.1.call-start = ((), (), s32[]{:S(2)}) async-start(), calls=%async_computation | async-start | bytes 11894784 | tf_op jit(solution)/shard_map/all_gather | solution.py:83
  6.5 16.3 %copy-start.17 = (f32[1,32,256]{2,1,0:T(8,128)S(1)}, f32[1,32,256]{2,1,0:T(8,128)}, u32[]{:S(2)}) copy-start(f32[1,32,256]{2,1,0:T(8,128)} %param.13) | copy-start | bytes 98308
  7.4 16.2 %copy-start.14 = (bf16[1,256,2048]{2,1,0:T(8,128)(2,1)S(1)}, bf16[1,256,2048]{2,1,0:T(8,128)(2,1)}, u32[]{:S(2)}) copy-start(bf16[1,256,2048]{2,1,0:T(8,128)(2,1)} %param.9) | copy-start | bytes 3145732
  7.4 4.2 %collective-permute-start.10 = (bf16[11,2048]{1,0:T(8,128)(2,1)S(1)}, bf16[11,2048]{1,0:T(8,128)(2,1)S(1)}, u32[]{:S(2)}, u32[]{:S(2)}) collective-permute-start(bf16[11,2048]{1,0:T(8,128)(2,1)S(1)} %select_bitcast_fusion.4), channel_id=1, source_target_pairs={{0,4},{4,0},{1,5},{5,1},{2,6},{6,2},{3,7},{7,3},{8,12},{12,8},{9,1... | collective-permute-start | bytes 135176 | tf_op jit(solution)/shard_map/ppermute | solution.py:21
  12.5 6.5 %collective-permute-start.11 = (bf16[2,11,2048]{2,1,0:T(8,128)(2,1)S(1)}, bf16[2,11,2048]{2,1,0:T(8,128)(2,1)S(1)}, u32[]{:S(2)}, u32[]{:S(2)}) collective-permute-start(bf16[2,11,2048]{2,1,0:T(8,128)(2,1)S(1)} %pad_maximum_fusion.6), channel_id=1, source_target_pairs={{0,1},{1,2},{2,3},{3,0},{4,5},{5,6},{6,7},{7,4},{8,9},{9,10},{10,1... | collective-permute-start | bytes 270344 | tf_op jit(solution)/shard_map/ppermute | solution.py:26
  12.6 8.3 %collective-permute-start.12 = (bf16[2,11,2048]{2,1,0:T(8,128)(2,1)S(1)}, bf16[2,11,2048]{2,1,0:T(8,128)(2,1)S(1)}, u32[]{:S(2)}, u32[]{:S(2)}) collective-permute-start(bf16[2,11,2048]{2,1,0:T(8,128)(2,1)S(1)} %pad_maximum_fusion.6), channel_id=1, source_target_pairs={{0,2},{1,3},{2,0},{3,1},{4,6},{5,7},{6,4},{7,5},{8,10},{9,11},{10,... | collective-permute-start | bytes 270344 | tf_op jit(solution)/shard_map/ppermute | solution.py:26
  14.8 6.8 %collective-permute-start.13 = (bf16[2,11,2048]{2,1,0:T(8,128)(2,1)S(1)}, bf16[2,11,2048]{2,1,0:T(8,128)(2,1)S(1)}, u32[]{:S(2)}, u32[]{:S(2)}) collective-permute-start(bf16[2,11,2048]{2,1,0:T(8,128)(2,1)S(1)} %pad_maximum_fusion.6), channel_id=1, source_target_pairs={{0,3},{1,0},{2,1},{3,2},{4,7},{5,4},{6,5},{7,6},{8,11},{9,8},{10,9... | collective-permute-start | bytes 270344 | tf_op jit(solution)/shard_map/ppermute | solution.py:26
  27.1 4.1 %collective-permute-start = (f32[2056,128]{1,0:T(8,128)}, f32[2056,128]{1,0:T(8,128)}, u32[]{:S(2)}, u32[]{:S(2)}) collective-permute-start(f32[2056,128]{1,0:T(8,128)} %select_maximum_fusion), channel_id=1, source_target_pairs={{0,4},{4,0},{1,5},{5,1},{2,6},{6,2},{3,7},{7,3},{8,12},{12,8},{9,1... | collective-permute-start | bytes 3158024 | tf_op jit(solution)/shard_map/ppermute | solution.py:21
  35.8 9.9 %collective-permute-start.1 = (bf16[1032,128]{1,0:T(8,128)(2,1)S(1)}, bf16[1032,128]{1,0:T(8,128)(2,1)S(1)}, u32[]{:S(2)}, u32[]{:S(2)}) collective-permute-start(bf16[1032,128]{1,0:T(8,128)(2,1)S(1)} %fusion.20), channel_id=1, source_target_pairs={{0,8},{8,0},{16,24},{24,16},{32,40},{40,32},{48,56},{56,48},{1,9},... | collective-permute-start | bytes 792584 | tf_op jit(solution)/shard_map/ppermute | solution.py:21
  45.9 71.5 %copy-start.5 = (bf16[1024,128]{1,0:T(8,128)(2,1)}, bf16[1024,128]{1,0:T(8,128)(2,1)S(1)}, u32[]{:S(2)}) copy-start(bf16[1024,128]{1,0:T(8,128)(2,1)S(1)} %slice.168) | copy-start | bytes 786436
  47.1 9.8 %collective-permute-start.2 = (bf16[520,128]{1,0:T(8,128)(2,1)S(1)}, bf16[520,128]{1,0:T(8,128)(2,1)S(1)}, u32[]{:S(2)}, u32[]{:S(2)}) collective-permute-start(bf16[520,128]{1,0:T(8,128)(2,1)S(1)} %fusion.31), channel_id=1, source_target_pairs={{0,16},{8,24},{16,0},{24,8},{32,48},{40,56},{48,32},{56,40},{1,17}... | collective-permute-start | bytes 399368 | tf_op jit(solution)/shard_map/ppermute | solution.py:21
  50.2 17.4 %copy-start.15 = (f32[256,256]{1,0:T(8,128)S(1)}, f32[256,256]{1,0:T(8,128)}, u32[]{:S(2)}) copy-start(f32[256,256]{1,0:T(8,128)} %fusion.37) | copy-start | bytes 786436
  56.9 19.9 %copy-start.18 = (f32[1,32]{1,0:T(1,128)}, f32[1,32]{1,0:T(1,128)S(1)}, u32[]{:S(2)}) copy-start(f32[1,32]{1,0:T(1,128)S(1)} %get-tuple-element.19) | copy-start | bytes 388
  56.9 19.9 %copy-start.22 = (f32[32]{0:T(128)}, f32[32]{0:T(128)S(1)}, u32[]{:S(2)}) copy-start(f32[32]{0:T(128)S(1)} %get-tuple-element.18) | copy-start | bytes 388
  58.2 18.5 %collective-permute-start.3 = (bf16[520,128]{1,0:T(8,128)(2,1)S(1)}, bf16[520,128]{1,0:T(8,128)(2,1)S(1)}, u32[]{:S(2)}, u32[]{:S(2)}) collective-permute-start(bf16[520,128]{1,0:T(8,128)(2,1)S(1)} %fusion.32), channel_id=1, source_target_pairs={{0,32},{8,40},{16,48},{24,56},{32,0},{40,8},{48,16},{56,24},{1,33}... | collective-permute-start | bytes 399368 | tf_op jit(solution)/shard_map/ppermute | solution.py:21
  78.2 14.2 %collective-permute-start.6 = (bf16[520,128]{1,0:T(8,128)(2,1)}, bf16[520,128]{1,0:T(8,128)(2,1)}, u32[]{:S(2)}, u32[]{:S(2)}) collective-permute-start(bf16[520,128]{1,0:T(8,128)(2,1)} %fusion.33), channel_id=1, source_target_pairs={{0,64},{64,0},{128,192},{1,65},{65,1},{129,193},{2,66},{66,2},{130... | collective-permute-start | bytes 399368 | tf_op jit(solution)/shard_map/ppermute | solution.py:21
  91.1 19.4 %collective-permute-start.4 = (bf16[2,8,64,128]{3,2,1,0:T(8,128)(2,1)}, bf16[2,8,64,128]{3,2,1,0:T(8,128)(2,1)}, u32[]{:S(2)}, u32[]{:S(2)}) collective-permute-start(bf16[2,8,64,128]{3,2,1,0:T(8,128)(2,1)} %pad_maximum_fusion.4), channel_id=1, source_target_pairs={{16,24},{24,16},{32,40},{40,32},{48,56},{56,48},{17,25},{25,17},{3... | collective-permute-start | bytes 786440 | tf_op jit(solution)/shard_map/ppermute | solution.py:21
  96.3 10.5 %collective-permute-start.7 = (bf16[520,128]{1,0:T(8,128)(2,1)S(1)}, bf16[520,128]{1,0:T(8,128)(2,1)S(1)}, u32[]{:S(2)}, u32[]{:S(2)}) collective-permute-start(bf16[520,128]{1,0:T(8,128)(2,1)S(1)} %fusion.34), channel_id=1, source_target_pairs={{0,128},{64,192},{1,129},{65,193},{2,130},{66,194},{3,131},{67,195... | collective-permute-start | bytes 399368 | tf_op jit(solution)/shard_map/ppermute | solution.py:21
  106.9 3.6 %collective-permute-start.8 = (bf16[2,8,64,128]{3,2,1,0:T(8,128)(2,1)S(1)}, bf16[2,8,64,128]{3,2,1,0:T(8,128)(2,1)S(1)}, u32[]{:S(2)}, u32[]{:S(2)}) collective-permute-start(bf16[2,8,64,128]{3,2,1,0:T(8,128)(2,1)S(1)} %pad_maximum_fusion.5), channel_id=1, source_target_pairs={{64,72},{72,64},{80,88},{88,80},{96,104},{104,96},{112,120},{120,1... | collective-permute-start | bytes 786440 | tf_op jit(solution)/shard_map/ppermute | solution.py:21
  114.7 6.3 %collective-permute-start.9 = (bf16[2,16,64,128]{3,2,1,0:T(8,128)(2,1)}, bf16[2,16,64,128]{3,2,1,0:T(8,128)(2,1)}, u32[]{:S(2)}, u32[]{:S(2)}) collective-permute-start(bf16[2,16,64,128]{3,2,1,0:T(8,128)(2,1)} %pad_maximum_fusion.2), channel_id=1, source_target_pairs={{0,4},{4,0},{1,5},{5,1},{2,6},{6,2},{3,7},{7,3},{8,12},{12,8},{9,1... | collective-permute-start | bytes 1572872 | tf_op jit(solution)/shard_map/ppermute | solution.py:21
  118.4 4.2 %collective-permute-start.5 = (bf16[3,16,64,128]{3,2,1,0:T(8,128)(2,1)}, bf16[3,16,64,128]{3,2,1,0:T(8,128)(2,1)}, u32[]{:S(2)}, u32[]{:S(2)}) collective-permute-start(bf16[3,16,64,128]{3,2,1,0:T(8,128)(2,1)} %maximum_maximum_fusion), channel_id=1, source_target_pairs={{0,4},{4,0},{1,5},{5,1},{2,6},{6,2},{3,7},{7,3},{8,12},{12,8},{9,1... | collective-permute-start | bytes 2359304 | tf_op jit(solution)/shard_map/ppermute | solution.py:21
  131.8 2.8 %collective-permute-start.14 = (bf16[256,2048]{1,0:T(8,128)(2,1)S(1)}, bf16[256,2048]{1,0:T(8,128)(2,1)S(1)}, u32[]{:S(2)}, u32[]{:S(2)}) collective-permute-start(bf16[256,2048]{1,0:T(8,128)(2,1)S(1)} %shard_map.91), channel_id=1, source_target_pairs={{0,4},{4,0},{1,5},{5,1},{2,6},{6,2},{3,7},{7,3},{8,12},{12,8},{9,1... | collective-permute-start | bytes 3145736 | tf_op jit(solution)/shard_map/ppermute | solution.py:21
  132.3 20.3 %copy-start.2 = (bf16[256,2048]{1,0:T(8,128)(2,1)S(1)}, bf16[256,2048]{1,0:T(8,128)(2,1)}, u32[]{:S(2)}) copy-start(bf16[256,2048]{1,0:T(8,128)(2,1)} %copy-done.1) | copy-start | bytes 3145732
  151.6 7.4 %collective-permute-start.15 = (f32[256,2816]{1,0:T(8,128)S(1)}, f32[256,2816]{1,0:T(8,128)S(1)}, u32[]{:S(2)}, u32[]{:S(2)}) collective-permute-start(f32[256,2816]{1,0:T(8,128)S(1)} %fusion.60), channel_id=1, source_target_pairs={{0,4},{4,0},{1,5},{5,1},{2,6},{6,2},{3,7},{7,3},{8,12},{12,8},{9,1... | collective-permute-start | bytes 8650760 | tf_op jit(solution)/shard_map/ppermute | solution.py:21
  (20 other events, 116.1 us)
Sparse Core Ops, SparseCore 0:
  22.9 122.3 all-gather.1
